TPU v7x, 32 devices: a whole 2x2x4 slice. The times are simulated.
32 devices in a mesh: groups: 2 (over x), seq: 16 (over z, y, core).
Axes of the slice: x: 2, y: 2, z: 4, core: 2. Of those that a mesh axis runs over, the one named last changes fastest.
Arguments:
- tokens: bfloat16 [128, 5120], P(('groups', 'seq')), parts along dimension 0, may hold values from -6 to 6
- out_grad: bfloat16 [128, 5120], P(('groups', 'seq')), parts along dimension 0, may hold values from -6 to 6
- ffn_out: bfloat16 [128, 5120], P(('groups', 'seq')), parts along dimension 0, may hold values from -6 to 6
- modulation: float32 [42, 3, 5120], P('groups'), parts along dimension 0, may hold values from -3 to 3
- in_weight: bfloat16 [5120, 13824], P(None, 'seq'), may hold values from -0.078125 to 0.078125
- in_bias: float32 [13824], P('seq'), may hold values from -4 to 4
- out_weight: bfloat16 [13824, 5120], P('seq'), may hold values from -0.0546875 to 0.0546875
- frame_ids: int32 [128], P('groups'), parts along dimension 0, may hold values from 0 to 20, never falling along the last dimension, each value on 1 to 6 neighbouring positions
- frame_slot: int32 [42], P('groups'), parts along dimension 0, may hold values from 0 to 31, as said below
Outputs:
- token_grad: bfloat16 [128, 5120], P(('groups', 'seq')), parts along dimension 0
- in_weight_grad: bfloat16 [10240, 13824], P('groups', 'seq'), parts along dimension 0
- out_weight_grad: bfloat16 [27648, 5120], P(('groups', 'seq')), parts along dimension 0
- frame_grads: float32 [64, 3, 5120], P(('groups', 'seq')), parts along dimension 0
There are 2 independent parts, one for each index of `groups`. A program takes and returns all parts, laid end to end along the dimension named above; an argument that names none is the same for every part. Nothing has to cross between parts.
Inputs may be any that keep to these rules, and one draw needn't show every extreme that they name: `frame_ids`: frames are runs of consecutive rows in order, each of 1 to 6 rows, one of exactly 6. `frame_slot`: distinct slots; the slot s belongs to index s // 2 of seq.
All inputs are finite; a program needn't handle non-finite values.
Results may differ from a plain program's by a relative error of at most 0.007.
Values may be sent and summed in bfloat16 or wider, within the bound.
A program may use at most 128 MiB of HBM per device.

v0:
```python
import jax
import jax.numpy as jnp
from jax import lax
from jax.sharding import PartitionSpec as P

EPSILON = 1e-06
HIGH = lax.Precision.HIGHEST


def gelu_tanh(value_in):
    return jax.nn.gelu(value_in, approximate=True)


def normalize(inputs):
    values = inputs.astype(jnp.float32)
    centred = values - jnp.mean(values, axis=1, keepdims=True)
    inverse_std = lax.rsqrt(jnp.mean(centred * centred, axis=1, keepdims=True) + EPSILON)
    return (centred * inverse_std, inverse_std)


def frame_rows(frame_index, modulation):
    frame_count = modulation.shape[0]
    one_hot = (frame_index[:, None] == jnp.arange(frame_count, dtype=jnp.int32)[None, :]).astype(
        jnp.float32
    )
    shift = jnp.dot(one_hot, modulation[:, 0, :], precision=HIGH)
    scale = jnp.dot(one_hot, modulation[:, 1, :], precision=HIGH)
    gate = jnp.dot(one_hot, modulation[:, 2, :], precision=HIGH)
    return (one_hot, shift, scale, gate)


def prepare(normed, shift, scale, gate, out_grad):
    modulated = (normed * (1.0 + scale) + shift).astype(jnp.bfloat16)
    gated_grad = (out_grad.astype(jnp.float32) * gate).astype(jnp.bfloat16)
    return (modulated, gated_grad)


def finish(mod_grad, normed, inverse_std, scale, out_grad):
    normed_grad = mod_grad * (1.0 + scale)
    mean_grad = jnp.mean(normed_grad, axis=1, keepdims=True)
    mean_proj = jnp.mean(normed_grad * normed, axis=1, keepdims=True)
    result = (
        out_grad.astype(jnp.float32) + (normed_grad - mean_grad - normed * mean_proj) * inverse_std
    )
    return result.astype(jnp.bfloat16)


def per_device(
    tokens, out_grad, ffn_out, modulation, in_weight, in_bias, out_weight, frame_ids, frame_slot
):
    local_rows = tokens.shape[0]
    feature_count = tokens.shape[1]
    frame_count = modulation.shape[0]
    devices = lax.axis_size("seq")
    my_index = lax.axis_index("seq")
    row_base = my_index * local_rows
    local_ids = lax.dynamic_slice_in_dim(frame_ids, row_base, local_rows, 0)
    one_hot, shift, scale, gate = frame_rows(local_ids, modulation)
    normed, inverse_std = normalize(tokens)
    modulated, gated_grad = prepare(normed, shift, scale, gate, out_grad)
    all_modulated, all_gated = (
        lax.all_gather(modulated, "seq", axis=0, tiled=True),
        lax.all_gather(gated_grad, "seq", axis=0, tiled=True),
    )
    hidden_pre = jnp.dot(all_modulated, in_weight, preferred_element_type=jnp.float32) + in_bias
    activated, pull_back = jax.vjp(gelu_tanh, hidden_pre)
    activated = activated.astype(jnp.bfloat16)
    out_weight_grad = jnp.einsum(
        "tf,td->fd", activated, all_gated, preferred_element_type=jnp.float32
    ).astype(jnp.bfloat16)
    act_grad = lax.dot_general(
        all_gated, out_weight, (((1,), (1,)), ((), ())), preferred_element_type=jnp.float32
    )
    hidden_grad = pull_back(act_grad)[0].astype(jnp.bfloat16)
    in_weight_grad = jnp.einsum(
        "td,tf->df", all_modulated, hidden_grad, preferred_element_type=jnp.float32
    ).astype(jnp.bfloat16)
    mod_grad = lax.psum_scatter(
        lax.dot_general(
            hidden_grad, in_weight, (((1,), (1,)), ((), ())), preferred_element_type=jnp.float32
        ),
        "seq",
        scatter_dimension=0,
        tiled=True,
    )
    token_grad = finish(mod_grad, normed, inverse_std, scale, out_grad)
    stacked = jnp.concatenate(
        [mod_grad, mod_grad * normed, out_grad.astype(jnp.float32) * ffn_out.astype(jnp.float32)],
        axis=1,
    )
    per_frame = lax.dot_general(one_hot, stacked, (((0,), (0,)), ((), ())), precision=HIGH)
    per_owner = (frame_count + devices - 1) // devices
    slot_total = per_owner * devices
    slot_hot = (frame_slot[:, None] == jnp.arange(slot_total, dtype=jnp.int32)[None, :]).astype(
        jnp.float32
    )
    spread = lax.dot_general(slot_hot, per_frame, (((0,), (0,)), ((), ())), precision=HIGH)
    owned_sums = lax.psum_scatter(spread, "seq", scatter_dimension=0, tiled=True)
    frame_grads = owned_sums.reshape(per_owner, 3, feature_count)
    return (token_grad, in_weight_grad, out_weight_grad, frame_grads)


def solution(mesh):
    in_specs = (
        P(("groups", "seq"), None),
        P(("groups", "seq"), None),
        P(("groups", "seq"), None),
        P("groups", None, None),
        P(None, "seq"),
        P("seq"),
        P("seq", None),
        P("groups"),
        P("groups"),
    )
    out_specs = (
        P(("groups", "seq"), None),
        P("groups", "seq"),
        P(("groups", "seq"), None),
        P(("groups", "seq"), None, None),
    )
    return jax.shard_map(
        per_device, mesh=mesh, in_specs=in_specs, out_specs=out_specs, check_vma=False
    )
```

profile of v0, /device:TPU:0, one launch (start us, length us, event | category | flops | bytes accessed | tf_op | source)
XLA Modules:
  0.0 273.9 jit_solution(14842176583258790259)
XLA Ops:
  7.2 0.0 all-reduce.5.cloned.1.call-start
  7.2 0.9 convert_reduce_fusion
  8.2 1.0 fusion.36
  9.2 0.7 dynamic_slice.3
  9.9 1.3 convolution_add_fusion.1
  11.2 1.3 fusion.3
  12.6 1.3 fusion.2
  13.9 25.1 %all-gather.1 = bf16[16,4,5120]{2,1,0:T(4,128)(2,1)S(1)} all-gather(bf16[1,4,5120]{2,1,0:T(4,128)(2,1)S(1)} %fusion.2), channel_id=1, replica_groups=mesh['groups'=2,'seq'=16] {'seq'}, dimensions={0}, use_global_device_ids=true | all-gather | bytes 696320 | tf_op jit(solution)/shard_map/all_gather | solution.py:62
  39.0 0.1 reshape.38
  39.2 19.2 %all-gather = bf16[16,4,5120]{2,1,0:T(4,128)(2,1)S(1)} all-gather(bf16[1,4,5120]{2,1,0:T(4,128)(2,1)S(1)} %fusion.3), channel_id=1, replica_groups=mesh['groups'=2,'seq'=16] {'seq'}, dimensions={0}, use_global_device_ids=true | all-gather | bytes 696320 | tf_op jit(solution)/shard_map/all_gather | solution.py:63
  58.4 0.1 reshape.36
  58.6 0.0 copy-start
  58.6 0.0 copy-start.4
  58.6 6.4 %fusion.50 = f32[64,864]{1,0:T(8,128)S(1)} fusion(bf16[64,5120]{1,0:T(8,128)(2,1)S(1)} %reshape.36, bf16[864,5120]{1,0:T(8,128)(2,1)} %param.15), kind=kOutput, calls=%fused_computation.71 | convolution fusion | flops 566231040 | bytes 9723904 | tf_op jit(solution)/shard_map/dot_general | solution.py:71
  65.0 0.0 copy-done
  65.0 0.0 copy-done.4
  65.0 2.8 %fusion.22 = (bf16[64,864]{1,0:T(8,128)(2,1)S(1)}, f32[64,864]{1,0:T(8,128)S(1)}) fusion(f32[64,864]{1,0:T(8,128)S(1)} %fusion.50, f32[864]{0:T(1024)S(1)} %copy-done.4, bf16[64,5120]{1,0:T(8,128)(2,1)S(1)} %reshape.38, bf16[5120,864]{0,1:T(8,128)(2,1)S(1)} %copy-done), kind=kOutput, calls=%fused_computation.30 | convolution fusion | flops 567392256 | bytes 10059136 | tf_op jit(solution)/shard_map/dot_general | solution.py:65
  67.9 0.0 copy-start.6
  67.9 0.0 copy-start.1
  67.9 0.0 copy-start.2
  67.9 0.0 copy-start.3
  67.9 2.8 %fusion.51 = f32[64,5120]{1,0:T(8,128)} fusion(bf16[64,864]{1,0:T(8,128)(2,1)S(1)} %get-tuple-element.23, bf16[5120,864]{0,1:T(8,128)(2,1)S(1)} %copy-done), kind=kOutput, calls=%fused_computation.72 | convolution fusion | flops 566231040 | bytes 10268672 | tf_op jit(solution)/shard_map/dot_general | solution.py:79
  70.7 0.0 copy-start.5
  70.7 0.0 all-reduce.5.cloned.1.call-update
  70.8 0.2 all-reduce.7.cloned.1.call-start
  71.0 0.0 copy-done.6
  71.0 0.6 dynamic-slice
  72.2 90.6 %all-reduce.5.cloned.1.call-done = f32[64,5120]{1,0:T(8,128)} async-done(((f32[64,5120]{1,0:T(8,128)}), f32[64,5120]{1,0:T(8,128)}) %all-reduce.5.cloned.1.call-update) | async-done | bytes 1310736
  162.9 0.0 copy-done.1
  162.9 1.0 fusion.29
  163.9 0.2 fusion.49
  164.1 0.0 copy-done.2
  164.1 0.0 copy-done.3
  164.1 0.7 convert_multiply_fusion
  164.9 0.9 fusion.10
  165.8 0.0 copy-done.5
  165.8 2.3 fusion.38
  168.1 0.0 all-reduce.7.cloned.1.call-update
  168.8 6.0 %convolution_convert_fusion.1 = bf16[5120,864]{0,1:T(8,128)(2,1)} fusion(bf16[64,5120]{1,0:T(8,128)(2,1)S(1)} %reshape.38, bf16[64,864]{1,0:T(8,128)(2,1)S(1)} %get-tuple-element.23), kind=kOutput, calls=%fused_computation.1 | convolution fusion | flops 570654720 | bytes 9613312 | tf_op jit(solution)/shard_map/td,tf->df/dot_general | solution.py:75
  174.8 6.1 %convolution_convert_fusion = bf16[864,5120]{1,0:T(8,128)(2,1)} fusion(bf16[64,5120]{1,0:T(8,128)(2,1)S(1)} %reshape.36, f32[64,864]{1,0:T(8,128)S(1)} %get-tuple-element.24), kind=kOutput, calls=%fused_computation | convolution fusion | flops 571152384 | bytes 9723904 | tf_op jit(solution)/shard_map/tf,td->fd/dot_general | solution.py:68
  180.9 84.4 %all-reduce.7.cloned.1.call-done = f32[32,15360]{1,0:T(8,128)} async-done(((f32[32,15360]{1,0:T(8,128)}), f32[32,15360]{1,0:T(8,128)}) %all-reduce.7.cloned.1.call-update) | async-done | bytes 1966096
  265.3 1.7 constant_dynamic-slice_fusion
  (3 shorter events, 0.0 us)
Async XLA Ops:
  7.2 155.7 %all-reduce.5.cloned.1.call-start = ((), (), s32[]{:S(2)}) async-start(), calls=%async_computation | async-start | bytes 2621440
  58.6 6.4 %copy-start = (bf16[5120,864]{0,1:T(8,128)(2,1)S(1)}, bf16[5120,864]{0,1:T(8,128)(2,1)}, u32[]{:S(2)}) copy-start(bf16[5120,864]{0,1:T(8,128)(2,1)} %param.13) | copy-start | bytes 26542084
  58.6 6.4 %copy-start.4 = (f32[864]{0:T(1024)S(1)}, f32[864]{0:T(1024)}, u32[]{:S(2)}) copy-start(f32[864]{0:T(1024)} %param.14) | copy-start | bytes 10372
  67.9 3.1 %copy-start.6 = (u32[32]{0:T(128)S(1)}, u32[32]{0:T(128)}, u32[]{:S(2)}) copy-start(u32[32]{0:T(128)} %constant.40) | copy-start | bytes 388
  67.9 95.0 %copy-start.1 = (bf16[4,5120]{1,0:T(4,128)(2,1)S(1)}, bf16[4,5120]{1,0:T(4,128)(2,1)}, u32[]{:S(2)}) copy-start(bf16[4,5120]{1,0:T(4,128)(2,1)} %param.9) | copy-start | bytes 122884
  67.9 96.2 %copy-start.2 = (bf16[4,5120]{1,0:T(4,128)(2,1)S(1)}, bf16[4,5120]{1,0:T(4,128)(2,1)}, u32[]{:S(2)}) copy-start(bf16[4,5120]{1,0:T(4,128)(2,1)} %param.10) | copy-start | bytes 122884
  67.9 96.2 %copy-start.3 = (bf16[4,5120]{1,0:T(4,128)(2,1)S(1)}, bf16[4,5120]{1,0:T(4,128)(2,1)}, u32[]{:S(2)}) copy-start(bf16[4,5120]{1,0:T(4,128)(2,1)} %param.11) | copy-start | bytes 122884
  70.7 95.0 %copy-start.5 = (s32[21]{0:T(128)S(1)}, s32[21]{0:T(128)}, u32[]{:S(2)}) copy-start(s32[21]{0:T(128)} %param.17) | copy-start | bytes 256
  70.8 194.6 %all-reduce.7.cloned.1.call-start = ((), (), s32[]{:S(2)}) async-start(), calls=%async_computation.1 | async-start | bytes 3932160
Sparse Core Ops, SparseCore 0:
  70.9 91.9 all-reduce.4
  168.3 97.0 all-reduce.6
where the time goes:
time: 274 us
  waiting for transfers between devices  175 us (64%)
  blocking collectives  44.3 us (16%)
  matrix products  31.4 us (11%)
  between operations  15.5 us (6%)
  other arithmetic  3.93 us (1%)
  local copies, waits for them, and re-layouts  3.38 us (1%)
    unnamed x4, waiting for transfers between devices  175 us
    all_gather x1, blocking collectives, per_device(): lax.all_gather(modulated, 'seq', axis=0, tiled=True)  25.1 us
    all_gather x1, blocking collectives, per_device(): lax.all_gather(gated_grad, 'seq', axis=0, tiled=True)  19.2 us
    dot_general x1, matrix products, per_device(): lax.dot_general(all_gated, out_weight, (((1,), (1,)), ((), ())), preferre...  6.39 us
    dot_general x1, matrix products, per_device(): jnp.einsum('tf,td->fd', activated, all_gated, preferred_element_type=jnp....  6.06 us
    dot_general x1, matrix products, per_device(): jnp.einsum('td,tf->df', all_modulated, hidden_grad, preferred_element_typ...  6.04 us
  transfers between devices with their start and end apart: 2, of which 2 were waited for; matrix products, arithmetic and copies ran while one was open for 5% of the time, Pallas kernels for 0%

commit v1 on v0

v1 whole, which is shorter than its diff:
```python
import functools

import jax
import jax.numpy as jnp
import numpy as np
from jax import lax
from jax.experimental import pallas as pl
from jax.experimental.pallas import tpu as pltpu
from jax.sharding import PartitionSpec as P

EPSILON = 1e-06
MESH = pl.DeviceIdType.MESH


def gelu_tanh(value_in):
    return jax.nn.gelu(value_in, approximate=True)


def normalize(inputs):
    values = inputs.astype(jnp.float32)
    centred = values - jnp.mean(values, axis=1, keepdims=True)
    inverse_std = lax.rsqrt(jnp.mean(centred * centred, axis=1, keepdims=True) + EPSILON)
    return (centred * inverse_std, inverse_std)


def position(lines):
    me = lax.axis_index("seq")
    return me, me // 4, (me // 2) % 2, me % 2


def device(line, side, core):
    return {"seq": (line * 2 + side) * 2 + core}


def greet(lines, line, side, core):
    barrier = pltpu.get_barrier_semaphore()
    for step in range(1, lines):
        pl.semaphore_signal(
            barrier, inc=1, device_id=device((line + step) % lines, side, core), device_id_type=MESH
        )
    pl.semaphore_signal(barrier, inc=1, device_id=device(line, 1 - side, core), device_id_type=MESH)
    pl.semaphore_signal(barrier, inc=1, device_id=device(line, side, 1 - core), device_id_type=MESH)
    pl.semaphore_wait(barrier, lines + 1)


def gather_kernel(lines, mine_ref, all_ref, line_send, side_send, core_send, recv):
    me, line, side, core = position(lines)
    greet(lines, line, side, core)

    def copy(source, block, send, where):
        return pltpu.make_async_remote_copy(
            src_ref=source,
            dst_ref=all_ref.at[block],
            send_sem=send,
            recv_sem=recv.at[block],
            device_id=where,
            device_id_type=MESH,
        )

    def arrived(block):
        copy(all_ref.at[block], block, line_send.at[0], device(line, side, 1 - core)).wait_recv()

    sent = []

    def send(source, block, sem, where):
        started = copy(source, block, sem, where)
        started.start()
        sent.append(started)

    for step in range(1, lines):
        send(mine_ref, me, line_send.at[step - 1], device((line + step) % lines, side, core))
    send(mine_ref, me, side_send.at[0], device(line, 1 - side, core))
    send(mine_ref, me, core_send.at[0], device(line, side, 1 - core))
    all_ref[me] = mine_ref[...]
    for step in range(1, lines):
        block = (((line - step + lines) % lines) * 2 + side) * 2 + core
        arrived(block)
        send(all_ref.at[block], block, side_send.at[step], device(line, 1 - side, core))
        send(all_ref.at[block], block, core_send.at[step], device(line, side, 1 - core))
    for step in range(lines):
        block = (((line - step + lines) % lines) * 2 + 1 - side) * 2 + core
        arrived(block)
        send(all_ref.at[block], block, core_send.at[lines + step], device(line, side, 1 - core))
    for step in range(lines):
        for other in range(2):
            arrived((((line - step + lines) % lines) * 2 + other) * 2 + 1 - core)
    for started in sent:
        started.wait_send()


def gather_blocks(block, n):
    lines = n // 4
    return pl.pallas_call(
        functools.partial(gather_kernel, lines),
        out_shape=jax.ShapeDtypeStruct((n,) + block.shape, block.dtype),
        in_specs=[pl.BlockSpec(memory_space=pltpu.VMEM)],
        out_specs=pl.BlockSpec(memory_space=pltpu.VMEM),
        scratch_shapes=[
            pltpu.SemaphoreType.DMA((lines,)),
            pltpu.SemaphoreType.DMA((lines,)),
            pltpu.SemaphoreType.DMA((2 * lines,)),
            pltpu.SemaphoreType.DMA((n,)),
        ],
        compiler_params=pltpu.CompilerParams(
            collective_id=0, has_side_effects=True, vmem_limit_bytes=32 * 2**20
        ),
        name="gather_rows",
    )(block)


def reduce_kernel(
    lines,
    parts_ref,
    out_ref,
    from_core,
    to_side,
    from_side,
    to_line,
    from_line,
    core_send,
    core_recv,
    side_send,
    side_recv,
    line_send,
    line_recv,
):
    me, line, side, core = position(lines)
    greet(lines, line, side, core)
    sent = []

    def send(source, target, send_sem, recv_sem, where):
        started = pltpu.make_async_remote_copy(
            src_ref=source,
            dst_ref=target,
            send_sem=send_sem,
            recv_sem=recv_sem,
            device_id=where,
            device_id_type=MESH,
        )
        started.start()
        sent.append(started)
        return started

    order = [(line + step) % lines for step in list(range(1, lines)) + [0]]
    core_copies = {}
    for away in (1, 0):
        for step, place in enumerate(order):
            other = 1 - side if away else side
            slot = away * lines + step
            core_copies[slot] = send(
                parts_ref.at[1 - core, other, place],
                from_core.at[slot],
                core_send.at[slot],
                core_recv.at[slot],
                device(line, side, 1 - core),
            )
    side_copies = []
    for step, place in enumerate(order):
        slot = lines + step
        core_copies[slot].wait_recv()
        to_side[step] = (
            parts_ref[core, 1 - side, place].astype(jnp.float32)
            + from_core[slot].astype(jnp.float32)
        ).astype(jnp.bfloat16)
        side_copies.append(
            send(
                to_side.at[step],
                from_side.at[step],
                side_send.at[step],
                side_recv.at[step],
                device(line, 1 - side, core),
            )
        )
    line_copies = []
    for step, place in enumerate(order):
        core_copies[step].wait_recv()
        side_copies[step].wait_recv()
        total = (
            parts_ref[core, side, place].astype(jnp.float32)
            + from_core[step].astype(jnp.float32)
            + from_side[step].astype(jnp.float32)
        )
        if step < lines - 1:
            to_line[step] = total.astype(jnp.bfloat16)
            line_copies.append(
                send(
                    to_line.at[step],
                    from_line.at[step],
                    line_send.at[step],
                    line_recv.at[step],
                    device(place, side, core),
                )
            )
        else:
            out_ref[...] = total
    for step in range(lines - 1):
        line_copies[step].wait_recv()
        out_ref[...] += from_line[step].astype(jnp.float32)
    for started in sent:
        started.wait_send()


def reduce_blocks(parts, n):
    lines = n // 4
    block = parts.shape[3:]
    return pl.pallas_call(
        functools.partial(reduce_kernel, lines),
        out_shape=jax.ShapeDtypeStruct(block, jnp.float32),
        in_specs=[pl.BlockSpec(memory_space=pltpu.VMEM)],
        out_specs=pl.BlockSpec(memory_space=pltpu.VMEM),
        scratch_shapes=[
            pltpu.VMEM((2 * lines,) + block, jnp.bfloat16),
            pltpu.VMEM((lines,) + block, jnp.bfloat16),
            pltpu.VMEM((lines,) + block, jnp.bfloat16),
            pltpu.VMEM((lines,) + block, jnp.bfloat16),
            pltpu.VMEM((lines,) + block, jnp.bfloat16),
            pltpu.SemaphoreType.DMA((2 * lines,)),
            pltpu.SemaphoreType.DMA((2 * lines,)),
            pltpu.SemaphoreType.DMA((lines,)),
            pltpu.SemaphoreType.DMA((lines,)),
            pltpu.SemaphoreType.DMA((lines,)),
            pltpu.SemaphoreType.DMA((lines,)),
        ],
        compiler_params=pltpu.CompilerParams(
            collective_id=1, has_side_effects=True, vmem_limit_bytes=32 * 2**20
        ),
        name="reduce_rows",
    )(parts)


def finish(mod_grad, normed, inverse_std, scale, out_grad):
    normed_grad = mod_grad * (1.0 + scale)
    mean_grad = jnp.mean(normed_grad, axis=1, keepdims=True)
    mean_proj = jnp.mean(normed_grad * normed, axis=1, keepdims=True)
    result = (
        out_grad.astype(jnp.float32) + (normed_grad - mean_grad - normed * mean_proj) * inverse_std
    )
    return result.astype(jnp.bfloat16)


def per_device(
    tokens, out_grad, ffn_out, modulation, in_weight, in_bias, out_weight, frame_ids, frame_slot
):
    rows, features = tokens.shape
    frame_count = modulation.shape[0]
    n = lax.axis_size("seq")
    lines = n // 4
    total_rows = rows * n
    half = features // 2
    row_base = lax.axis_index("seq") * rows

    one_hot = frame_ids[:, None] == jnp.arange(frame_count, dtype=jnp.int32)[None, :]
    row_slot = jnp.sum(jnp.where(one_hot, frame_slot[None, :], 0), axis=1)
    one_hot = one_hot.astype(jnp.float32)

    def spread(which):
        return jnp.dot(one_hot, modulation[:, which, :], precision=lax.Precision.HIGH)

    shift, scale, gate = spread(0), spread(1), spread(2)

    mine = jnp.concatenate([tokens[:, :half], out_grad[:, :half], tokens[:, half:], out_grad[:, half:]], axis=0)
    gathered = gather_blocks(mine, n).reshape(n, 2, 2, rows, half)

    def whole(which):
        return jnp.concatenate(
            [gathered[:, side, which].reshape(total_rows, half) for side in range(2)], axis=1
        )

    all_tokens, all_out_grad = whole(0), whole(1)
    normed, inverse_std = normalize(all_tokens)
    modulated = (normed * (1.0 + scale) + shift).astype(jnp.bfloat16)
    gated_grad = (all_out_grad.astype(jnp.float32) * gate).astype(jnp.bfloat16)

    hidden_pre = jnp.dot(modulated, in_weight, preferred_element_type=jnp.float32) + in_bias
    activated, pull_back = jax.vjp(gelu_tanh, hidden_pre)
    activated = activated.astype(jnp.bfloat16)
    act_grad = lax.dot_general(
        gated_grad, out_weight, (((1,), (1,)), ((), ())), preferred_element_type=jnp.float32
    )
    hidden_grad = pull_back(act_grad)[0].astype(jnp.bfloat16)
    partial = lax.dot_general(
        hidden_grad, in_weight, (((1,), (1,)), ((), ())), preferred_element_type=jnp.float32
    )

    per_owner = (frame_count + n - 1) // n
    kinds = rows + 3 * per_owner
    kinds += kinds % 2
    owner = np.arange(n).reshape(lines, 2, 2).transpose(2, 1, 0).reshape(n, 1)
    token_of = np.full((n, kinds), -1, np.int32)
    token_of[:, :rows] = owner * rows + np.arange(rows)
    slot_of = np.full((3, n, kinds), -1, np.int32)
    for kind in range(3):
        first = rows + kind * per_owner
        slot_of[kind, :, first : first + per_owner] = owner * per_owner + np.arange(per_owner)
    token_of = token_of.reshape(-1, 1)
    slot_of = slot_of.reshape(3, -1, 1)
    my_slot = lax.dynamic_slice_in_dim(row_slot, row_base, rows, 0)
    choose = jnp.concatenate(
        [
            (token_of == np.arange(total_rows, dtype=np.int32)[None, :])
            | (slot_of[0] == row_slot[None, :]),
            slot_of[1] == row_slot[None, :],
            slot_of[2] == my_slot[None, :],
        ],
        axis=1,
    ).astype(jnp.bfloat16)
    gate_rows = out_grad.astype(jnp.float32) * ffn_out.astype(jnp.float32)
    terms = jnp.concatenate(
        [
            partial.astype(jnp.bfloat16),
            (partial * normed).astype(jnp.bfloat16),
            gate_rows.astype(jnp.bfloat16),
        ],
        axis=0,
    )
    parts = jnp.dot(choose, terms, preferred_element_type=jnp.float32).astype(jnp.bfloat16)
    cuts = 8
    parts = parts.reshape(2, 2, lines, kinds, cuts, features // cuts).transpose(0, 1, 2, 4, 3, 5)
    parts = parts.reshape(2, 2, lines, cuts * kinds, features // cuts)
    sums = reduce_blocks(parts, n)
    sums = sums.reshape(cuts, kinds, features // cuts).transpose(1, 0, 2).reshape(kinds, features)

    out_weight_grad = jnp.einsum(
        "tf,td->fd", activated, gated_grad, preferred_element_type=jnp.float32
    ).astype(jnp.bfloat16)
    in_weight_grad = jnp.einsum(
        "td,tf->df", modulated, hidden_grad, preferred_element_type=jnp.float32
    ).astype(jnp.bfloat16)

    mod_grad = sums[:rows]
    my_scale = lax.dynamic_slice_in_dim(scale, row_base, rows, 0)
    my_normed, my_inverse_std = normalize(tokens)
    token_grad = finish(mod_grad, my_normed, my_inverse_std, my_scale, out_grad)
    frame_grads = sums[rows : rows + 3 * per_owner].reshape(3, per_owner, features)
    return (token_grad, in_weight_grad, out_weight_grad, frame_grads.transpose(1, 0, 2))


def solution(mesh):
    in_specs = (
        P(("groups", "seq"), None),
        P(("groups", "seq"), None),
        P(("groups", "seq"), None),
        P("groups", None, None),
        P(None, "seq"),
        P("seq"),
        P("seq", None),
        P("groups"),
        P("groups"),
    )
    out_specs = (
        P(("groups", "seq"), None),
        P("groups", "seq"),
        P(("groups", "seq"), None),
        P(("groups", "seq"), None, None),
    )
    return jax.shard_map(
        per_device, mesh=mesh, in_specs=in_specs, out_specs=out_specs, check_vma=False
    )
```

time: 274 us -> 79.2 us (0.29)
  waiting for transfers between devices: 175 us -> 0 us
  blocking collectives: 44.3 us -> 0 us
  Pallas kernels: 0 us -> 36.8 us
  between operations: 15.5 us -> 0.95 us
  other arithmetic: 3.93 us -> 7.71 us
    unnamed x4 -> x0, waiting for transfers between devices: 175 us -> none
    all_gather x2 -> x0, blocking collectives: 44.3 us -> none  [the longest x1 25.1 us: per_device(): lax.all_gather(modulated, 'seq', axis=0, tiled=True)]
    pallas_call x0 -> x2, Pallas kernels: none -> 36.8 us  [the longest x1 18.7 us: reduce_blocks(): pl.pallas_call(functools.partial(reduce_kernel, lines), out_shape=jax.Sha...]
    dot_general x9 -> x8, matrix products: 28.5 us -> 27.6 us  [the longest x1 6.39 us: per_device(): lax.dot_general(gated_grad, out_weight, (((1,), (1,)), ((), ())), preferr...]
  transfers between devices with their start and end apart: 2 -> 0, of which waited for: 2 -> 0; matrix products, arithmetic and copies ran while one was open for 5% -> 0% of each run, Pallas kernels for 0% -> 0%
where the time goes in v1:
time: 79.2 us; the launch traced here: 78.7 us
  Pallas kernels  36.8 us (46%)
  matrix products  29.4 us (37%)
  other arithmetic  7.71 us (10%)
  local copies, waits for them, and re-layouts  3.97 us (5%)
  between operations  0.95 us (1%)
    pallas_call x1, Pallas kernels, reduce_blocks(): pl.pallas_call(functools.partial(reduce_kernel, lines), out_shape=jax.Sha...  18.7 us
    pallas_call x1, Pallas kernels, gather_blocks(): pl.pallas_call(functools.partial(gather_kernel, lines), out_shape=jax.Sha...  18.1 us
    dot_general x1, matrix products, per_device(): lax.dot_general(gated_grad, out_weight, (((1,), (1,)), ((), ())), preferr...  6.39 us
    dot_general x1, matrix products, per_device(): jnp.einsum('tf,td->fd', activated, gated_grad, preferred_element_type=jnp...  6.25 us
    dot_general x1, matrix products, per_device(): jnp.einsum('td,tf->df', modulated, hidden_grad, preferred_element_type=jn...  6.04 us
    dot_general x3, matrix products, spread(): jnp.dot(one_hot, modulation[:, which, :], precision=lax.Precision.HIGH)  5.45 us
    dot_general x1, matrix products, per_device(): jnp.dot(modulated, in_weight, preferred_element_type=jnp.float32) + in_bias  2.8 us
    dot_general x1, matrix products, per_device(): lax.dot_general(hidden_grad, in_weight, (((1,), (1,)), ((), ())), preferr...  1.75 us

profile of v1, /device:TPU:0, one launch (start us, length us, event | category | flops | bytes accessed | tf_op | source)
XLA Modules:
  0.0 78.7 jit_solution(13723060484848636906)
XLA Ops:
  0.6 0.8 select_reduce_fusion
  1.4 0.1 dynamic_slice.6
  1.5 0.9 %convert_reduce_fusion.1 = f32[4]{0:T(128)S(1)} fusion(bf16[4,5120]{1,0:T(4,128)(2,1)} %param.13), kind=kLoop, calls=%fused_computation.49 | loop fusion | flops 40956 | bytes 40976 | tf_op jit(solution)/shard_map/reduce_sum | solution.py:21
  2.4 1.0 %fusion.43 = f32[4]{0:T(128)S(1)} fusion(bf16[4,5120]{1,0:T(4,128)(2,1)} %param.13, f32[4]{0:T(128)S(1)} %broadcast_multiply_fusion.1), kind=kLoop, calls=%fused_computation.59 | loop fusion | flops 81916 | bytes 40992 | tf_op jit(solution)/shard_map/reduce_sum | solution.py:22
  3.4 0.8 broadcast_compare_fusion
  4.2 0.9 %compare_or_fusion = (pred[160,64]{1,0:T(32,128)(4,1)S(1)}, pred[160,64]{1,0:T(32,128)(4,1)S(1)}) fusion(pred[160,64]{1,0:T(32,128)(4,1)} %constant.47.clone, s32[64]{0:T(128)S(1)} %select_reduce_fusion, s32[160]{0:T(256)} %constant.55, s32[160]{0:T(256)} %constant.56), kind=kLoop, calls=%fused_computation.64 | loop fusion | flops 30720 | bytes 32256 | tf_op jit(solution)/shard_map/or | solution.py:300
  5.1 0.8 %fusion.44 = bf16[4,5120]{1,0:T(4,128)(2,1)S(1)} fusion(bf16[4,5120]{1,0:T(4,128)(2,1)} %param.14, bf16[4,5120]{1,0:T(4,128)(2,1)} %param.15), kind=kLoop, calls=%fused_computation.60 | loop fusion | flops 81920 | bytes 122880 | tf_op jit(solution)/shard_map/convert_element_type | solution.py:312
  5.9 0.8 %fusion.58 = (bf16[4,2560]{1,0:T(4,128)(2,1)S(1)}, bf16[4,2560]{1,0:T(4,128)(2,1)S(1)}, bf16[4,2560]{1,0:T(4,128)(2,1)S(1)}, bf16[4,2560]{1,0:T(4,128)(2,1)S(1)}) fusion(bf16[4,5120]{1,0:T(4,128)(2,1)} %param.13, bf16[4,5120]{1,0:T(4,128)(2,1)} %param.14), kind=kLoop, calls=%fused_computation.87 | loop fusion | bytes 163840 | tf_op jit(solution)/shard_map/slice | solution.py:261
  6.7 0.1 pad_maximum_fusion.1.mine_ref
  6.8 18.1 %gather_rows.1 = bf16[16,16,2560]{2,1,0:T(8,128)(2,1)S(1)} custom-call(bf16[16,2560]{1,0:T(8,128)(2,1)S(1)} %pad_maximum_fusion.1.mine_ref), custom_call_target="tpu_custom_call" | custom-call | tf_op jit(solution)/shard_map/gather_rows/pallas_call | solution.py:93
  24.9 0.3 reshape.64
  25.2 0.0 slice-start
  25.2 0.5 fusion.57
  25.7 0.1 reshape_squeeze.12
  25.8 0.1 reshape_squeeze.15
  25.9 0.0 copy-start.3
  25.9 0.1 reshape_squeeze.14
  25.9 0.2 convert_reduce_fusion
  26.2 0.3 fusion.12
  26.5 0.1 reshape_squeeze.13
  26.6 0.0 copy-done.3
  26.6 0.0 slice-start.1
  26.6 1.8 %fusion = bf16[64,5120]{1,0:T(8,128)(2,1)S(1)} fusion(bf16[64,2560]{1,0:T(8,128)(2,1)S(1)} %reshape_squeeze.13, bf16[64,2560]{1,0:T(8,128)(2,1)S(1)} %reshape_squeeze.12, f32[21,3,5120]{2,0,1:T(8,128)} %param.16, s32[64]{0:T(128)S(1)} %copy-done.3), kind=kOutput, calls=%fused_computation.5 | convolution fusion | flops 43255104 | bytes 1802496 | tf_op jit(solution)/shard_map/dot_general | solution.py:257
  28.4 0.0 copy-start
  28.4 0.0 slice-start.2
  28.4 6.4 %fusion.60 = f32[64,864]{1,0:T(8,128)S(1)} fusion(bf16[64,5120]{1,0:T(8,128)(2,1)S(1)} %fusion, bf16[864,5120]{1,0:T(8,128)(2,1)} %param.19), kind=kOutput, calls=%fused_computation.89 | convolution fusion | flops 566231040 | bytes 9723904 | tf_op jit(solution)/shard_map/dot_general | solution.py:277
  34.8 0.0 copy-done
  34.8 1.6 %fusion.14 = f32[64,5120]{1,0:T(8,128)} fusion(f32[21,3,5120]{2,0,1:T(8,128)S(1)} %copy-done, s32[64]{0:T(128)S(1)} %copy-done.3), kind=kOutput, calls=%fused_computation.23 | convolution fusion | flops 41289024 | bytes 1802752 | tf_op jit(solution)/shard_map/dot_general | solution.py:257
  36.5 0.0 copy-start.4
  36.5 2.1 %fusion.1 = bf16[64,5120]{1,0:T(8,128)(2,1)S(1)} fusion(f32[64,5120]{1,0:T(8,128)} %fusion.14, f32[64]{0:T(128)S(1)} %add_rsqrt_fusion.1, f32[64]{0:T(128)S(1)} %broadcast_multiply_fusion.3, f32[21,3,5120]{2,0,1:T(8,128)S(1)} %copy-done, s32[64]{0:T(128)S(1)} %copy-done.3, bf16[64,2560]{1,0:T(8,128)(2,1)S(1)} %reshape_squeeze.15, ...), kind=kOutput, calls=%fused_computation.6 | convolution fusion | flops 44565824 | bytes 3114496 | tf_op jit(solution)/shard_map/dot_general | solution.py:257
  38.5 0.0 slice-done
  38.5 0.0 slice-done.1
  38.6 0.0 slice-done.2
  38.6 0.0 copy-done.4
  38.6 2.8 %fusion.26 = (bf16[64,864]{1,0:T(8,128)(2,1)S(1)}, f32[64,864]{1,0:T(8,128)S(1)}) fusion(f32[64,864]{1,0:T(8,128)S(1)} %fusion.60, f32[864]{0:T(1024)S(1)} %copy-done.4, bf16[64,5120]{1,0:T(8,128)(2,1)S(1)} %fusion.1, bf16[5120,864]{0,1:T(8,128)(2,1)S(1)} %bitcast.28), kind=kOutput, calls=%fused_computation.37 | convolution fusion | flops 567392256 | bytes 10059136 | tf_op jit(solution)/shard_map/dot_general | solution.py:274
  41.4 1.8 %fusion.56 = (bf16[64,5120]{1,0:T(8,128)(2,1)S(1)}, bf16[64,5120]{1,0:T(8,128)(2,1)S(1)}) fusion(f32[64]{0:T(128)S(1)} %add_rsqrt_fusion.1, f32[64]{0:T(128)S(1)} %broadcast_multiply_fusion.3, bf16[64,2560]{1,0:T(8,128)(2,1)S(1)} %reshape_squeeze.15, bf16[64,2560]{1,0:T(8,128)(2,1)S(1)} %reshape_squeeze.14, bf16[64,864]{1,0:T(8,128)(2,1)S(1)} %get-tuple-element.19, ...), kind=kOutput, calls=%fused_computation.85 | convolution fusion | flops 569180160 | bytes 10924544 | tf_op jit(solution)/shard_map/dot_general | solution.py:281
  43.1 0.7 convolution_convert_fusion.2
  43.8 0.3 copy.27
  44.1 0.6 copy.24
  44.7 0.2 copy.25.parts_ref
  44.9 0.0 copy-start.1
  45.0 18.7 %reduce_rows.1 = f32[80,640]{1,0:T(8,128)S(1)} custom-call(bf16[2,2,4,80,640]{4,3,2,1,0:T(8,128)(2,1)S(1)} %copy.25.parts_ref), custom_call_target="tpu_custom_call" | custom-call | tf_op jit(solution)/shard_map/reduce_rows/pallas_call | solution.py:206
  63.6 0.0 copy-start.2
  63.8 0.7 reshape.68
  64.5 0.0 copy-done.1
  64.5 1.2 %fusion.55 = (f32[4]{0:T(128)S(1)}, f32[4]{0:T(128)S(1)}, f32[4,5120]{1,0:T(4,128)S(1)}) fusion(f32[4]{0:T(128)S(1)} %add_rsqrt_fusion, f32[4]{0:T(128)S(1)} %broadcast_multiply_fusion.1, bf16[4,5120]{1,0:T(4,128)(2,1)S(1)} %copy-done.1, f32[4,5120]{1,0:T(4,128)S(1)} %bitcast.34, f32[64,5120]{1,0:T(8,128)} %fusion.14, s32[]{:T(128)S(6)} %select_n.9), kind=kLoop, calls=%fused_computation.84 | loop fusion | flops 163832 | bytes 286788 | tf_op jit(solution)/shard_map/reduce_sum | solution.py:233
  65.7 0.0 copy-done.2
  65.7 0.7 fusion.45
  66.4 6.3 %convolution_convert_fusion = bf16[864,5120]{1,0:T(8,128)(2,1)} fusion(bf16[64,5120]{1,0:T(8,128)(2,1)S(1)} %fusion, f32[64,864]{1,0:T(8,128)S(1)} %get-tuple-element.20), kind=kOutput, calls=%fused_computation | convolution fusion | flops 571152384 | bytes 9723904 | tf_op jit(solution)/shard_map/tf,td->fd/dot_general | solution.py:323
  72.7 6.0 %convolution_convert_fusion.1 = bf16[5120,864]{0,1:T(8,128)(2,1)} fusion(bf16[64,5120]{1,0:T(8,128)(2,1)S(1)} %fusion.1, bf16[64,864]{1,0:T(8,128)(2,1)S(1)} %get-tuple-element.19), kind=kOutput, calls=%fused_computation.1 | convolution fusion | flops 570654720 | bytes 9613312 | tf_op jit(solution)/shard_map/td,tf->df/dot_general | solution.py:326
  (11 shorter events, 0.1 us)
Async XLA Ops:
  25.2 13.3 %slice-start = ((s8[8847360]{0:T(1024)(128)(4,1)}), s8[458752]{0:T(1024)(128)(4,1)S(1)}, s32[]{:S(2)}) async-start(s8[8847360]{0:T(1024)(128)(4,1)} %bitcast.27), calls=%async_computation | async-start | bytes 917504
  25.9 0.8 copy-start.3
  26.6 11.9 %slice-start.1 = ((s8[8847360]{0:T(1024)(128)(4,1)}), s8[4194304]{0:T(1024)(128)(4,1)S(1)}, s32[]{:S(2)}) async-start(s8[8847360]{0:T(1024)(128)(4,1)} %bitcast.27), calls=%async_computation.1 | async-start | bytes 8388608
  28.4 6.4 %copy-start = (f32[21,3,5120]{2,0,1:T(8,128)S(1)}, f32[21,3,5120]{2,0,1:T(8,128)}, u32[]{:S(2)}) copy-start(f32[21,3,5120]{2,0,1:T(8,128)} %param.16) | copy-start | bytes 3870724
  28.4 10.1 %slice-start.2 = ((s8[8847360]{0:T(1024)(128)(4,1)}), s8[4194304]{0:T(1024)(128)(4,1)S(1)}, s32[]{:S(2)}) async-start(s8[8847360]{0:T(1024)(128)(4,1)} %bitcast.27), calls=%async_computation.2 | async-start | bytes 8388608
  36.5 2.1 %copy-start.4 = (f32[864]{0:T(1024)S(1)}, f32[864]{0:T(1024)}, u32[]{:S(2)}) copy-start(f32[864]{0:T(1024)} %param.18) | copy-start | bytes 10372
  44.9 19.5 %copy-start.1 = (bf16[4,5120]{1,0:T(4,128)(2,1)S(1)}, bf16[4,5120]{1,0:T(4,128)(2,1)}, u32[]{:S(2)}) copy-start(bf16[4,5120]{1,0:T(4,128)(2,1)} %param.13) | copy-start | bytes 122884
  63.6 2.0 %copy-start.2 = (bf16[4,5120]{1,0:T(4,128)(2,1)S(1)}, bf16[4,5120]{1,0:T(4,128)(2,1)}, u32[]{:S(2)}) copy-start(bf16[4,5120]{1,0:T(4,128)(2,1)} %param.14) | copy-start | bytes 122884

commit v2 on v1

--- a/solution.py
+++ b/solution.py
@@ -43,66 +43,89 @@
     pl.semaphore_wait(barrier, lines + 1)
 
 
-def gather_kernel(lines, mine_ref, all_ref, line_send, side_send, core_send, recv):
+def gather_kernel(lines, pieces, mine_ref, all_ref, line_send, side_send, core_send, recv):
     me, line, side, core = position(lines)
     greet(lines, line, side, core)
-
-    def copy(source, block, send, where):
+    sent = []
+
+    def copy(source, block, piece, send, where):
         return pltpu.make_async_remote_copy(
             src_ref=source,
-            dst_ref=all_ref.at[block],
-            send_sem=send,
-            recv_sem=recv.at[block],
+            dst_ref=all_ref.at[block, piece],
+            send_sem=send.at[piece],
+            recv_sem=recv.at[block, piece],
             device_id=where,
             device_id_type=MESH,
         )
 
-    def arrived(block):
-        copy(all_ref.at[block], block, line_send.at[0], device(line, side, 1 - core)).wait_recv()
-
-    sent = []
-
-    def send(source, block, sem, where):
-        started = copy(source, block, sem, where)
+    def arrived(block, piece):
+        copy(
+            all_ref.at[block, piece], block, piece, core_send.at[0], device(line, side, 1 - core)
+        ).wait_recv()
+
+    def send(source, block, piece, sem, where):
+        started = copy(source, block, piece, sem, where)
         started.start()
         sent.append(started)
 
-    for step in range(1, lines):
-        send(mine_ref, me, line_send.at[step - 1], device((line + step) % lines, side, core))
-    send(mine_ref, me, side_send.at[0], device(line, 1 - side, core))
-    send(mine_ref, me, core_send.at[0], device(line, side, 1 - core))
+    for piece in range(pieces):
+        for step in range(1, lines):
+            send(
+                mine_ref.at[piece],
+                me,
+                piece,
+                line_send.at[step - 1],
+                device((line + step) % lines, side, core),
+            )
+        send(mine_ref.at[piece], me, piece, side_send.at[0], device(line, 1 - side, core))
+        send(mine_ref.at[piece], me, piece, core_send.at[0], device(line, side, 1 - core))
     all_ref[me] = mine_ref[...]
-    for step in range(1, lines):
-        block = (((line - step + lines) % lines) * 2 + side) * 2 + core
-        arrived(block)
-        send(all_ref.at[block], block, side_send.at[step], device(line, 1 - side, core))
-        send(all_ref.at[block], block, core_send.at[step], device(line, side, 1 - core))
-    for step in range(lines):
-        block = (((line - step + lines) % lines) * 2 + 1 - side) * 2 + core
-        arrived(block)
-        send(all_ref.at[block], block, core_send.at[lines + step], device(line, side, 1 - core))
-    for step in range(lines):
-        for other in range(2):
-            arrived((((line - step + lines) % lines) * 2 + other) * 2 + 1 - core)
+
+    def across(piece):
+        for step in range(lines):
+            block = (((line - step + lines) % lines) * 2 + 1 - side) * 2 + core
+            arrived(block, piece)
+            send(
+                all_ref.at[block, piece],
+                block,
+                piece,
+                core_send.at[lines + step],
+                device(line, side, 1 - core),
+            )
+
+    for piece in range(pieces):
+        for step in range(1, lines):
+            block = (((line - step + lines) % lines) * 2 + side) * 2 + core
+            arrived(block, piece)
+            source = all_ref.at[block, piece]
+            send(source, block, piece, side_send.at[step], device(line, 1 - side, core))
+            send(source, block, piece, core_send.at[step], device(line, side, 1 - core))
+        if piece:
+            across(piece - 1)
+    across(pieces - 1)
+    for piece in range(pieces):
+        for step in range(lines):
+            for other in range(2):
+                arrived((((line - step + lines) % lines) * 2 + other) * 2 + 1 - core, piece)
     for started in sent:
         started.wait_send()
 
 
 def gather_blocks(block, n):
-    lines = n // 4
+    lines, pieces = n // 4, block.shape[0]
     return pl.pallas_call(
-        functools.partial(gather_kernel, lines),
+        functools.partial(gather_kernel, lines, pieces),
         out_shape=jax.ShapeDtypeStruct((n,) + block.shape, block.dtype),
         in_specs=[pl.BlockSpec(memory_space=pltpu.VMEM)],
         out_specs=pl.BlockSpec(memory_space=pltpu.VMEM),
         scratch_shapes=[
-            pltpu.SemaphoreType.DMA((lines,)),
-            pltpu.SemaphoreType.DMA((lines,)),
-            pltpu.SemaphoreType.DMA((2 * lines,)),
-            pltpu.SemaphoreType.DMA((n,)),
+            pltpu.SemaphoreType.DMA((lines, pieces)),
+            pltpu.SemaphoreType.DMA((lines, pieces)),
+            pltpu.SemaphoreType.DMA((2 * lines, pieces)),
+            pltpu.SemaphoreType.DMA((n, pieces)),
         ],
         compiler_params=pltpu.CompilerParams(
-            collective_id=0, has_side_effects=True, vmem_limit_bytes=32 * 2**20
+            collective_id=0, has_side_effects=True, vmem_limit_bytes=8 * 2**20
         ),
         name="gather_rows",
     )(block)
@@ -222,10 +245,41 @@
             pltpu.SemaphoreType.DMA((lines,)),
         ],
         compiler_params=pltpu.CompilerParams(
-            collective_id=1, has_side_effects=True, vmem_limit_bytes=32 * 2**20
+            collective_id=1, has_side_effects=True, vmem_limit_bytes=20 * 2**20
         ),
         name="reduce_rows",
     )(parts)
+
+
+def product_kernel(activated_ref, gated_ref, hidden_ref, modulated_ref, out_ref, in_ref):
+    for left_ref, right_ref, target_ref in (
+        (activated_ref, gated_ref, out_ref),
+        (hidden_ref, modulated_ref, in_ref),
+    ):
+        target_ref[...] = lax.dot_general(
+            left_ref[...],
+            right_ref[...],
+            (((0,), (0,)), ((), ())),
+            preferred_element_type=jnp.float32,
+        ).astype(jnp.bfloat16)
+
+
+def weight_products(activated, gated_grad, hidden_grad, modulated):
+    (total_rows, hidden), features = activated.shape, modulated.shape[1]
+    width = 512
+    left = pl.BlockSpec((total_rows, hidden), lambda index: (0, 0))
+    right = pl.BlockSpec((total_rows, width), lambda index: (0, index))
+    target = pl.BlockSpec((hidden, width), lambda index: (0, index))
+    shape = jax.ShapeDtypeStruct((hidden, features), jnp.bfloat16)
+    return pl.pallas_call(
+        product_kernel,
+        grid=(features // width,),
+        out_shape=(shape, shape),
+        in_specs=[left, right, left, right],
+        out_specs=(target, target),
+        compiler_params=pltpu.CompilerParams(vmem_limit_bytes=24 * 2**20),
+        name="weight_products",
+    )(activated, gated_grad, hidden_grad, modulated)
 
 
 def finish(mod_grad, normed, inverse_std, scale, out_grad):
@@ -247,6 +301,7 @@
     lines = n // 4
     total_rows = rows * n
     half = features // 2
+    pieces = 4
     row_base = lax.axis_index("seq") * rows
 
     one_hot = frame_ids[:, None] == jnp.arange(frame_count, dtype=jnp.int32)[None, :]
@@ -259,7 +314,8 @@
     shift, scale, gate = spread(0), spread(1), spread(2)
 
     mine = jnp.concatenate([tokens[:, :half], out_grad[:, :half], tokens[:, half:], out_grad[:, half:]], axis=0)
-    gathered = gather_blocks(mine, n).reshape(n, 2, 2, rows, half)
+    mine = mine.reshape(4 * rows, pieces, half // pieces).transpose(1, 0, 2)
+    gathered = gather_blocks(mine, n).transpose(0, 2, 1, 3).reshape(n, 2, 2, rows, half)
 
     def whole(which):
         return jnp.concatenate(
@@ -320,12 +376,8 @@
     sums = reduce_blocks(parts, n)
     sums = sums.reshape(cuts, kinds, features // cuts).transpose(1, 0, 2).reshape(kinds, features)
 
-    out_weight_grad = jnp.einsum(
-        "tf,td->fd", activated, gated_grad, preferred_element_type=jnp.float32
-    ).astype(jnp.bfloat16)
-    in_weight_grad = jnp.einsum(
-        "td,tf->df", modulated, hidden_grad, preferred_element_type=jnp.float32
-    ).astype(jnp.bfloat16)
+    out_weight_grad, in_weight_grad = weight_products(activated, gated_grad, hidden_grad, modulated)
+    in_weight_grad = in_weight_grad.T
 
     mod_grad = sums[:rows]
     my_scale = lax.dynamic_slice_in_dim(scale, row_base, rows, 0)

time: 79.2 us -> 81.7 us (1.032)
  matrix products: 29.4 us -> 18.3 us
  Pallas kernels: 36.8 us -> 47.4 us
  local copies, waits for them, and re-layouts: 3.97 us -> 5.54 us
  other arithmetic: 7.71 us -> 9.03 us
    dot_general x2 -> x0, matrix products: 12.3 us -> none  [the longest x1 6.25 us: per_device(): jnp.einsum('tf,td->fd', activated, gated_grad, preferred_element_type=jnp...]
    pallas_call x1 -> x2, Pallas kernels: 18.1 us -> 28.5 us  [the longest x1 19.7 us: gather_blocks(): pl.pallas_call(functools.partial(gather_kernel, lines, pieces), out_shape...]
    dot_general x1, matrix products: 2.8 us -> 6.38 us  [per_device(): jnp.dot(modulated, in_weight, preferred_element_type=jnp.float32) + in_bias]
    dot_general x3, matrix products: 5.45 us -> 3.01 us  [spread(): jnp.dot(one_hot, modulation[:, which, :], precision=lax.Precision.HIGH)]
    rsqrt x2, other arithmetic: 0.02 us -> 1.08 us  [normalize(): lax.rsqrt(jnp.mean(centred * centred, axis=1, keepdims=True) + EPSILON)]
    reduce_sum x1, other arithmetic: 1.17 us -> 0.22 us  [finish(): mean_grad = jnp.mean(normed_grad, axis=1, keepdims=True)]
where the time goes in v2:
time: 81.7 us; the launch traced here: 81.3 us
  Pallas kernels  47.4 us (58%)
  matrix products  18.3 us (22%)
  other arithmetic  9.03 us (11%)
  local copies, waits for them, and re-layouts  5.54 us (7%)
  between operations  1.06 us (1%)
    pallas_call x1, Pallas kernels, gather_blocks(): pl.pallas_call(functools.partial(gather_kernel, lines, pieces), out_shape...  19.7 us
    pallas_call x1, Pallas kernels, reduce_blocks(): pl.pallas_call(functools.partial(reduce_kernel, lines), out_shape=jax.Sha...  18.9 us
    pallas_call x1, Pallas kernels, weight_products(): pl.pallas_call(product_kernel, grid=(features // width,), out_shape=(shap...  8.75 us
    dot_general x1, matrix products, per_device(): lax.dot_general(gated_grad, out_weight, (((1,), (1,)), ((), ())), preferr...  6.39 us
    dot_general x1, matrix products, per_device(): jnp.dot(modulated, in_weight, preferred_element_type=jnp.float32) + in_bias  6.38 us
    dot_general x3, matrix products, spread(): jnp.dot(one_hot, modulation[:, which, :], precision=lax.Precision.HIGH)  3.01 us
    dot_general x1, matrix products, per_device(): lax.dot_general(hidden_grad, in_weight, (((1,), (1,)), ((), ())), preferr...  1.82 us

profile of v2, /device:TPU:0, one launch (start us, length us, event | category | flops | bytes accessed | tf_op | source)
XLA Modules:
  0.0 81.3 jit_solution(2345771291023471890)
XLA Ops:
  0.6 0.8 select_reduce_fusion
  1.4 0.1 dynamic_slice.6
  1.5 0.9 %convert_reduce_fusion.1 = f32[4]{0:T(128)S(1)} fusion(bf16[4,5120]{1,0:T(4,128)(2,1)} %param.13), kind=kLoop, calls=%fused_computation.43 | loop fusion | flops 40956 | bytes 40976 | tf_op jit(solution)/shard_map/reduce_sum | solution.py:21
  2.4 1.0 %fusion.39 = f32[4]{0:T(128)S(1)} fusion(bf16[4,5120]{1,0:T(4,128)(2,1)} %param.13, f32[4]{0:T(128)S(1)} %broadcast_multiply_fusion.1), kind=kLoop, calls=%fused_computation.53 | loop fusion | flops 81916 | bytes 40992 | tf_op jit(solution)/shard_map/reduce_sum | solution.py:22
  3.4 0.5 add_rsqrt_fusion
  3.9 1.4 %broadcast_compare_fusion = pred[160,4]{1,0:T(32,128)(4,1)} fusion(s32[4]{0:T(128)S(1)} %dynamic_slice.6, s32[160]{0:T(256)} %constant.57), kind=kLoop, calls=%fused_computation.60 | loop fusion | flops 640 | bytes 1296 | tf_op jit(solution)/shard_map/eq | solution.py:359
  5.3 1.5 %compare_or_fusion = (pred[160,64]{1,0:T(32,128)(4,1)}, pred[160,64]{1,0:T(32,128)(4,1)}) fusion(pred[160,64]{1,0:T(32,128)(4,1)} %constant.47.clone, s32[64]{0:T(128)S(1)} %select_reduce_fusion, s32[160]{0:T(256)} %constant.55, s32[160]{0:T(256)} %constant.56), kind=kLoop, calls=%fused_computation.59 | loop fusion | flops 30720 | bytes 32256 | tf_op jit(solution)/shard_map/or | solution.py:356
  6.8 0.8 %fusion.40 = bf16[4,5120]{1,0:T(4,128)(2,1)S(1)} fusion(bf16[4,5120]{1,0:T(4,128)(2,1)} %param.14, bf16[4,5120]{1,0:T(4,128)(2,1)} %param.15), kind=kLoop, calls=%fused_computation.54 | loop fusion | flops 81920 | bytes 122880 | tf_op jit(solution)/shard_map/convert_element_type | solution.py:368
  7.6 0.8 %fusion.50 = (bf16[4,2560]{1,0:T(4,128)(2,1)S(1)}, bf16[4,2560]{1,0:T(4,128)(2,1)S(1)}, bf16[4,2560]{1,0:T(4,128)(2,1)S(1)}, bf16[4,2560]{1,0:T(4,128)(2,1)S(1)}) fusion(bf16[4,5120]{1,0:T(4,128)(2,1)} %param.13, bf16[4,5120]{1,0:T(4,128)(2,1)} %param.14), kind=kLoop, calls=%fused_computation.78 | loop fusion | bytes 163840 | tf_op jit(solution)/shard_map/slice | solution.py:316
  8.4 0.1 pad_maximum_fusion.1
  8.5 19.7 %gather_rows.1 = bf16[16,4,16,640]{3,2,1,0:T(8,128)(2,1)S(1)} custom-call(bf16[4,16,640]{2,1,0:T(8,128)(2,1)S(1)} %bitcast.44), custom_call_target="tpu_custom_call" | custom-call | tf_op jit(solution)/shard_map/gather_rows/pallas_call | solution.py:116
  28.3 0.6 copy.37
  28.9 0.5 reshape.68
  29.4 0.1 fusion.49
  29.5 0.3 copy.38
  29.8 0.1 reshape_squeeze.12
  29.9 0.3 copy.41
  30.1 0.1 reshape_squeeze.15
  30.2 0.3 copy.40
  30.5 0.1 reshape_squeeze.14
  30.6 0.0 copy-start.6
  30.6 0.2 convert_reduce_fusion
  30.8 0.3 fusion.12
  31.1 0.6 add_rsqrt_fusion.1
  31.7 0.3 copy.39
  32.0 0.1 reshape_squeeze.13
  32.0 0.0 copy-done.6
  32.0 0.0 copy-start
  32.1 1.7 %fusion.gated_ref = bf16[64,5120]{1,0:T(8,128)(2,1)S(1)} fusion(bf16[64,2560]{1,0:T(8,128)(2,1)S(1)} %reshape_squeeze.13, bf16[64,2560]{1,0:T(8,128)(2,1)S(1)} %reshape_squeeze.12, f32[21,3,5120]{2,0,1:T(8,128)} %param.16, s32[64]{0:T(128)S(1)} %copy-done.6), kind=kOutput, calls=%fused_computation.3 | convolution fusion | flops 43255104 | bytes 1802496 | tf_op jit(solution)/shard_map/dot_general | solution.py:312
  33.8 0.0 copy-start.7
  33.8 0.0 slice-start
  33.8 0.0 slice-start.1
  33.8 6.4 %fusion.52 = f32[64,864]{1,0:T(8,128)S(1)} fusion(bf16[64,5120]{1,0:T(8,128)(2,1)S(1)} %fusion.gated_ref, bf16[864,5120]{1,0:T(8,128)(2,1)} %param.19), kind=kOutput, calls=%fused_computation.80 | convolution fusion | flops 566231040 | bytes 9723904 | tf_op jit(solution)/shard_map/dot_general | solution.py:333
  40.2 0.0 copy-done
  40.2 0.0 copy-done.7
  40.2 0.0 copy-start.10
  40.3 0.6 fusion.14
  40.8 0.1 copy-done.10
  40.9 0.7 fusion.1.modulated_ref
  41.6 0.0 copy-done.8
  41.6 0.0 slice-start.2
  41.6 6.4 %multiply_convert_fusion = (bf16[64,864]{1,0:T(8,128)(2,1)S(1)}, bf16[64,864]{1,0:T(8,128)(2,1)S(1)}) fusion(f32[64,864]{1,0:T(8,128)S(1)} %fusion.52, f32[864]{0:T(1024)S(1)} %copy-done.8, bf16[64,5120]{1,0:T(8,128)(2,1)S(1)} %fusion.1.modulated_ref, bf16[5120,864]{0,1:T(8,128)(2,1)} %param.17), kind=kOutput, calls=%fused_computation.36 | convolution fusion | flops 567502848 | bytes 9948544 | tf_op jit(solution)/shard_map/dot_general | solution.py:330
  48.0 0.0 slice-done
  48.0 0.0 slice-done.1
  48.1 0.0 copy-start.3
  48.1 0.0 copy-start.4
  48.1 0.0 copy-start.5
  48.1 1.8 %fusion.48 = (bf16[64,5120]{1,0:T(8,128)(2,1)S(1)}, bf16[64,5120]{1,0:T(8,128)(2,1)S(1)}) fusion(f32[64]{0:T(128)S(1)} %copy-done.10, f32[64]{0:T(128)S(1)} %broadcast_multiply_fusion.3, bf16[64,2560]{1,0:T(8,128)(2,1)S(1)} %reshape_squeeze.15, bf16[64,2560]{1,0:T(8,128)(2,1)S(1)} %reshape_squeeze.14, bf16[64,864]{1,0:T(8,128)(2,1)S(1)} %get-tuple-element.18.hidden_ref, ...), kind=kOutput, calls=%fused_computation.76 | convolution fusion | flops 569180160 | bytes 10924544 | tf_op jit(solution)/shard_map/dot_general | solution.py:337
  49.9 0.0 copy-done.3
  49.9 0.0 copy-done.4
  50.0 0.0 copy-done.5
  50.0 0.7 convolution_convert_fusion
  50.6 0.3 copy.46
  50.9 0.6 copy.42
  51.5 0.2 copy.43.parts_ref
  51.8 0.0 copy-start.1
  51.8 0.0 copy-start.9
  51.8 18.9 %reduce_rows.1 = f32[80,640]{1,0:T(8,128)S(1)} custom-call(bf16[2,2,4,80,640]{4,3,2,1,0:T(8,128)(2,1)S(1)} %copy.43.parts_ref), custom_call_target="tpu_custom_call" | custom-call | tf_op jit(solution)/shard_map/reduce_rows/pallas_call | solution.py:229
  70.7 0.0 copy-start.2
  70.8 0.7 reshape.72
  71.5 0.0 copy-done.1
  71.5 0.2 fusion.47
  71.8 0.7 fusion.41
  72.5 8.7 %weight_products.1 = (bf16[864,5120]{1,0:T(8,128)(2,1)}, bf16[864,5120]{1,0:T(8,128)(2,1)}) custom-call(bf16[64,864]{1,0:T(8,128)(2,1)S(1)} %get-tuple-element.17.activated_ref, bf16[64,5120]{1,0:T(8,128)(2,1)S(1)} %fusion.gated_ref, bf16[64,864]{1,0:T(8,128)(2,1)S(1)} %get-tuple-element.18.hidden_ref, bf16[64,5120]{1,0:T(8,128)(2,1)S(1)} %fusion.1.modulated_ref), custom_call_target="tpu_custom_call" | custom-call | tf_op jit(solution)/shard_map/weight_products/pallas_call | solution.py:274
  (14 shorter events, 0.1 us)
Async XLA Ops:
  30.6 1.5 %copy-start.6 = (s32[64]{0:T(128)S(1)}, s32[64]{0:T(128)}, u32[]{:S(2)}) copy-start(s32[64]{0:T(128)} %param.20) | copy-start | bytes 772
  32.0 8.2 %copy-start = (f32[21,3,5120]{2,0,1:T(8,128)S(1)}, f32[21,3,5120]{2,0,1:T(8,128)}, u32[]{:S(2)}) copy-start(f32[21,3,5120]{2,0,1:T(8,128)} %param.16) | copy-start | bytes 3870724
  33.8 6.4 %copy-start.7 = (s32[64]{0:T(128)S(1)}, s32[64]{0:T(128)}, u32[]{:S(2)}) copy-start(s32[64]{0:T(128)} %param.20) | copy-start | bytes 772
  33.8 14.2 %slice-start = ((s8[8847360]{0:T(1024)(128)(4,1)}), s8[4194304]{0:T(1024)(128)(4,1)S(1)}, s32[]{:S(2)}) async-start(s8[8847360]{0:T(1024)(128)(4,1)} %bitcast.45), calls=%async_computation | async-start | bytes 8388608
  33.8 14.2 %slice-start.1 = ((s8[8847360]{0:T(1024)(128)(4,1)}), s8[4194304]{0:T(1024)(128)(4,1)S(1)}, s32[]{:S(2)}) async-start(s8[8847360]{0:T(1024)(128)(4,1)} %bitcast.45), calls=%async_computation.1 | async-start | bytes 8388608
  40.2 0.6 copy-start.10
  40.9 0.7 copy-start.8
  41.6 6.4 %slice-start.2 = ((s8[8847360]{0:T(1024)(128)(4,1)}), s8[458752]{0:T(1024)(128)(4,1)S(1)}, s32[]{:S(2)}) async-start(s8[8847360]{0:T(1024)(128)(4,1)} %bitcast.45), calls=%async_computation.2 | async-start | bytes 917504
  48.1 1.9 %copy-start.3 = (pred[160,4]{1,0:T(32,128)(4,1)S(1)}, pred[160,4]{1,0:T(32,128)(4,1)}, u32[]{:S(2)}) copy-start(pred[160,4]{1,0:T(32,128)(4,1)} %broadcast_compare_fusion) | copy-start | bytes 1924
  48.1 1.9 %copy-start.4 = (pred[160,64]{1,0:T(32,128)(4,1)S(1)}, pred[160,64]{1,0:T(32,128)(4,1)}, u32[]{:S(2)}) copy-start(pred[160,64]{1,0:T(32,128)(4,1)} %get-tuple-element.23) | copy-start | bytes 30724
  48.1 1.9 %copy-start.5 = (pred[160,64]{1,0:T(32,128)(4,1)S(1)}, pred[160,64]{1,0:T(32,128)(4,1)}, u32[]{:S(2)}) copy-start(pred[160,64]{1,0:T(32,128)(4,1)} %get-tuple-element.24) | copy-start | bytes 30724
  51.8 19.8 %copy-start.1 = (bf16[4,5120]{1,0:T(4,128)(2,1)S(1)}, bf16[4,5120]{1,0:T(4,128)(2,1)}, u32[]{:S(2)}) copy-start(bf16[4,5120]{1,0:T(4,128)(2,1)} %param.13) | copy-start | bytes 122884
  51.8 19.8 %copy-start.9 = (f32[4]{0:T(128)S(1)}, f32[4]{0:T(128)}, u32[]{:S(2)}) copy-start(f32[4]{0:T(128)} %add_rsqrt_fusion) | copy-start | bytes 52
  70.7 1.1 %copy-start.2 = (bf16[4,5120]{1,0:T(4,128)(2,1)S(1)}, bf16[4,5120]{1,0:T(4,128)(2,1)}, u32[]{:S(2)}) copy-start(bf16[4,5120]{1,0:T(4,128)(2,1)} %param.14) | copy-start | bytes 122884

commit v3 on v1

--- a/solution.py
+++ b/solution.py
@@ -12,10 +12,6 @@
 MESH = pl.DeviceIdType.MESH
 
 
-def gelu_tanh(value_in):
-    return jax.nn.gelu(value_in, approximate=True)
-
-
 def normalize(inputs):
     values = inputs.astype(jnp.float32)
     centred = values - jnp.mean(values, axis=1, keepdims=True)
@@ -43,7 +39,36 @@
     pl.semaphore_wait(barrier, lines + 1)
 
 
-def gather_kernel(lines, mine_ref, all_ref, line_send, side_send, core_send, recv):
+def middle_kernel(
+    lines,
+    mine_ref,
+    pick_ref,
+    ids_ref,
+    modulation_ref,
+    in_weight_hbm,
+    bias_ref,
+    out_weight_hbm,
+    modulated_ref,
+    gated_ref,
+    activated_ref,
+    hidden_ref,
+    terms_ref,
+    all_ref,
+    in_weight_ref,
+    out_weight_ref,
+    tokens_ref,
+    line_send,
+    side_send,
+    core_send,
+    recv,
+    load,
+):
+    loads = [
+        pltpu.make_async_copy(in_weight_hbm, in_weight_ref, load.at[0]),
+        pltpu.make_async_copy(out_weight_hbm, out_weight_ref, load.at[1]),
+    ]
+    for started in loads:
+        started.start()
     me, line, side, core = position(lines)
     greet(lines, line, side, core)
 
@@ -87,25 +112,129 @@
     for started in sent:
         started.wait_send()
 
-
-def gather_blocks(block, n):
+    n, block_rows, half = all_ref.shape
+    total_rows, features = tokens_ref.shape
+    width = half // 2
+    flat = all_ref[...].reshape(n * block_rows, half)
+    frames = lax.broadcasted_iota(jnp.int32, (total_rows, modulation_ref.shape[1]), 1)
+    one_hot = (ids_ref[...] == frames).astype(jnp.float32).astype(jnp.bfloat16)
+
+    def picked(which, column):
+        place = column % half
+        return jnp.dot(
+            pick_ref[2 * (column // half) + which],
+            flat[:, place : place + width],
+            preferred_element_type=jnp.float32,
+        )
+
+    def spread(which, column):
+        values = modulation_ref[which, :, column : column + width]
+        high = values.astype(jnp.bfloat16)
+        rest = values - high.astype(jnp.float32)
+        low = rest.astype(jnp.bfloat16)
+        lowest = (rest - low.astype(jnp.float32)).astype(jnp.bfloat16)
+        total = jnp.dot(one_hot, lowest, preferred_element_type=jnp.float32)
+        total = total + jnp.dot(one_hot, low, preferred_element_type=jnp.float32)
+        return total + jnp.dot(one_hot, high, preferred_element_type=jnp.float32)
+
+    columns = range(0, features, width)
+    total = jnp.zeros((total_rows, 1), jnp.float32)
+    for column in columns:
+        values = picked(0, column)
+        tokens_ref[:, column : column + width] = values
+        total = total + jnp.sum(values, axis=1, keepdims=True)
+        gated = picked(1, column) * spread(2, column)
+        gated_ref[:, column : column + width] = gated.astype(jnp.bfloat16)
+    mean = total / features
+    total = jnp.zeros((total_rows, 1), jnp.float32)
+    for column in columns:
+        centred = tokens_ref[:, column : column + width] - mean
+        total = total + jnp.sum(centred * centred, axis=1, keepdims=True)
+    inverse_std = lax.rsqrt(total / features + EPSILON)
+    for column in columns:
+        normed = (tokens_ref[:, column : column + width] - mean) * inverse_std
+        tokens_ref[:, column : column + width] = normed
+        modulated = normed * (1.0 + spread(1, column)) + spread(0, column)
+        modulated_ref[:, column : column + width] = modulated.astype(jnp.bfloat16)
+
+    across_last = (((1,), (1,)), ((), ()))
+    loads[0].wait()
+    value = (
+        lax.dot_general(
+            modulated_ref[...],
+            in_weight_ref[...],
+            across_last,
+            preferred_element_type=jnp.float32,
+        )
+        + bias_ref[...]
+    )
+    root = np.float32(np.sqrt(2.0 / np.pi))
+    cubic = np.float32(0.044715)
+    square = value * value
+    bend = jnp.tanh(root * (value + cubic * (square * value)))
+    activated_ref[...] = (value * (0.5 * (1.0 + bend))).astype(jnp.bfloat16)
+    slope = 0.5 * (1.0 + bend) + (0.5 * value) * (1.0 - bend * bend) * (
+        root * (1.0 + 3.0 * cubic * square)
+    )
+    loads[1].wait()
+    act_grad = lax.dot_general(
+        gated_ref[...], out_weight_ref[...], across_last, preferred_element_type=jnp.float32
+    )
+    hidden_ref[...] = (act_grad * slope).astype(jnp.bfloat16)
+    for column in columns:
+        partial = jnp.dot(
+            hidden_ref[...],
+            in_weight_ref[:, column : column + width],
+            preferred_element_type=jnp.float32,
+        )
+        terms_ref[:total_rows, column : column + width] = partial.astype(jnp.bfloat16)
+        terms_ref[total_rows:, column : column + width] = (
+            partial * tokens_ref[:, column : column + width]
+        ).astype(jnp.bfloat16)
+
+
+def middle(block, pick, frame_ids, modulation, in_weight, in_bias, out_weight, n):
     lines = n // 4
+    total_rows = frame_ids.shape[0]
+    hidden, features = in_weight.shape
+    vmem = pl.BlockSpec(memory_space=pltpu.VMEM)
+    hbm = pl.BlockSpec(memory_space=pl.ANY)
+    shapes = (
+        (total_rows, features),
+        (total_rows, features),
+        (total_rows, hidden),
+        (total_rows, hidden),
+        (2 * total_rows, features),
+    )
     return pl.pallas_call(
-        functools.partial(gather_kernel, lines),
-        out_shape=jax.ShapeDtypeStruct((n,) + block.shape, block.dtype),
-        in_specs=[pl.BlockSpec(memory_space=pltpu.VMEM)],
-        out_specs=pl.BlockSpec(memory_space=pltpu.VMEM),
+        functools.partial(middle_kernel, lines),
+        out_shape=tuple(jax.ShapeDtypeStruct(shape, jnp.bfloat16) for shape in shapes),
+        in_specs=[vmem, vmem, vmem, vmem, hbm, vmem, hbm],
+        out_specs=(vmem,) * 5,
         scratch_shapes=[
+            pltpu.VMEM((n,) + block.shape, block.dtype),
+            pltpu.VMEM((hidden, features), jnp.bfloat16),
+            pltpu.VMEM((hidden, features), jnp.bfloat16),
+            pltpu.VMEM((total_rows, features), jnp.float32),
             pltpu.SemaphoreType.DMA((lines,)),
             pltpu.SemaphoreType.DMA((lines,)),
             pltpu.SemaphoreType.DMA((2 * lines,)),
             pltpu.SemaphoreType.DMA((n,)),
+            pltpu.SemaphoreType.DMA((2,)),
         ],
         compiler_params=pltpu.CompilerParams(
-            collective_id=0, has_side_effects=True, vmem_limit_bytes=32 * 2**20
+            collective_id=0, has_side_effects=True, vmem_limit_bytes=56 * 2**20
         ),
-        name="gather_rows",
-    )(block)
+        name="gather_and_middle",
+    )(
+        block,
+        pick,
+        frame_ids[:, None],
+        modulation.transpose(1, 0, 2),
+        in_weight,
+        in_bias[None, :],
+        out_weight,
+    )
 
 
 def reduce_kernel(
@@ -222,10 +351,41 @@
             pltpu.SemaphoreType.DMA((lines,)),
         ],
         compiler_params=pltpu.CompilerParams(
-            collective_id=1, has_side_effects=True, vmem_limit_bytes=32 * 2**20
+            collective_id=1, has_side_effects=True, vmem_limit_bytes=20 * 2**20
         ),
         name="reduce_rows",
     )(parts)
+
+
+def product_kernel(activated_ref, gated_ref, hidden_ref, modulated_ref, out_ref, in_ref):
+    for left_ref, right_ref, target_ref in (
+        (activated_ref, gated_ref, out_ref),
+        (hidden_ref, modulated_ref, in_ref),
+    ):
+        target_ref[...] = lax.dot_general(
+            left_ref[...],
+            right_ref[...],
+            (((0,), (0,)), ((), ())),
+            preferred_element_type=jnp.float32,
+        ).astype(jnp.bfloat16)
+
+
+def weight_products(activated, gated_grad, hidden_grad, modulated):
+    (total_rows, hidden), features = activated.shape, modulated.shape[1]
+    width = 512
+    left = pl.BlockSpec((total_rows, hidden), lambda index: (0, 0))
+    right = pl.BlockSpec((total_rows, width), lambda index: (0, index))
+    target = pl.BlockSpec((hidden, width), lambda index: (0, index))
+    shape = jax.ShapeDtypeStruct((hidden, features), jnp.bfloat16)
+    return pl.pallas_call(
+        product_kernel,
+        grid=(features // width,),
+        out_shape=(shape, shape),
+        in_specs=[left, right, left, right],
+        out_specs=(target, target),
+        compiler_params=pltpu.CompilerParams(vmem_limit_bytes=24 * 2**20),
+        name="weight_products",
+    )(activated, gated_grad, hidden_grad, modulated)
 
 
 def finish(mod_grad, normed, inverse_std, scale, out_grad):
@@ -253,33 +413,12 @@
     row_slot = jnp.sum(jnp.where(one_hot, frame_slot[None, :], 0), axis=1)
     one_hot = one_hot.astype(jnp.float32)
 
-    def spread(which):
-        return jnp.dot(one_hot, modulation[:, which, :], precision=lax.Precision.HIGH)
-
-    shift, scale, gate = spread(0), spread(1), spread(2)
-
     mine = jnp.concatenate([tokens[:, :half], out_grad[:, :half], tokens[:, half:], out_grad[:, half:]], axis=0)
-    gathered = gather_blocks(mine, n).reshape(n, 2, 2, rows, half)
-
-    def whole(which):
-        return jnp.concatenate(
-            [gathered[:, side, which].reshape(total_rows, half) for side in range(2)], axis=1
-        )
-
-    all_tokens, all_out_grad = whole(0), whole(1)
-    normed, inverse_std = normalize(all_tokens)
-    modulated = (normed * (1.0 + scale) + shift).astype(jnp.bfloat16)
-    gated_grad = (all_out_grad.astype(jnp.float32) * gate).astype(jnp.bfloat16)
-
-    hidden_pre = jnp.dot(modulated, in_weight, preferred_element_type=jnp.float32) + in_bias
-    activated, pull_back = jax.vjp(gelu_tanh, hidden_pre)
-    activated = activated.astype(jnp.bfloat16)
-    act_grad = lax.dot_general(
-        gated_grad, out_weight, (((1,), (1,)), ((), ())), preferred_element_type=jnp.float32
-    )
-    hidden_grad = pull_back(act_grad)[0].astype(jnp.bfloat16)
-    partial = lax.dot_general(
-        hidden_grad, in_weight, (((1,), (1,)), ((), ())), preferred_element_type=jnp.float32
+    source = np.arange(total_rows) // rows * 4 * rows + np.arange(total_rows) % rows
+    pick = np.stack([source + kind * rows for kind in range(4)])[:, :, None]
+    pick = jnp.asarray(pick == np.arange(4 * total_rows), jnp.bfloat16)
+    modulated, gated_grad, activated, hidden_grad, terms = middle(
+        mine, pick, frame_ids, modulation, in_weight.T, in_bias, out_weight, n
     )
 
     per_owner = (frame_count + n - 1) // n
@@ -307,8 +446,7 @@
     gate_rows = out_grad.astype(jnp.float32) * ffn_out.astype(jnp.float32)
     terms = jnp.concatenate(
         [
-            partial.astype(jnp.bfloat16),
-            (partial * normed).astype(jnp.bfloat16),
+            terms,
             gate_rows.astype(jnp.bfloat16),
         ],
         axis=0,
@@ -320,15 +458,12 @@
     sums = reduce_blocks(parts, n)
     sums = sums.reshape(cuts, kinds, features // cuts).transpose(1, 0, 2).reshape(kinds, features)
 
-    out_weight_grad = jnp.einsum(
-        "tf,td->fd", activated, gated_grad, preferred_element_type=jnp.float32
-    ).astype(jnp.bfloat16)
-    in_weight_grad = jnp.einsum(
-        "td,tf->df", modulated, hidden_grad, preferred_element_type=jnp.float32
-    ).astype(jnp.bfloat16)
+    out_weight_grad, in_weight_grad = weight_products(activated, gated_grad, hidden_grad, modulated)
+    in_weight_grad = in_weight_grad.T
 
     mod_grad = sums[:rows]
-    my_scale = lax.dynamic_slice_in_dim(scale, row_base, rows, 0)
+    my_hot = lax.dynamic_slice_in_dim(one_hot, row_base, rows, 0)
+    my_scale = jnp.dot(my_hot, modulation[:, 1, :], precision=lax.Precision.HIGHEST)
     my_normed, my_inverse_std = normalize(tokens)
     token_grad = finish(mod_grad, my_normed, my_inverse_std, my_scale, out_grad)
     frame_grads = sums[rows : rows + 3 * per_owner].reshape(3, per_owner, features)

time: 79.2 us -> 76.2 us (0.962)
  matrix products: 29.4 us -> 3.52 us
  Pallas kernels: 36.8 us -> 58.5 us
  local copies, waits for them, and re-layouts: 3.97 us -> 5.46 us
    dot_general x8 -> x1, matrix products: 28.7 us -> 1.56 us  [per_device(): jnp.dot(my_hot, modulation[:, 1, :], precision=lax.Precision.HIGHEST)]
    pallas_call x1 -> x2, Pallas kernels: 18.1 us -> 39.9 us  [the longest x1 31.1 us: middle(): pl.pallas_call(functools.partial(middle_kernel, lines), out_shape=tuple((...]
    broadcast_in_dim x0 -> x2, local copies, waits for them, and re-layouts: none -> 2.63 us  [the longest x1 1.36 us: per_device(): frame_ids[:, None] == jnp.arange(frame_count, dtype=jnp.int32)[None, :]]
    dot_general x1, matrix products: 0.66 us -> 1.96 us  [per_device(): jnp.dot(choose, terms, preferred_element_type=jnp.float32)]
    reduce_sum x1 -> x0, other arithmetic: 1.17 us -> none  [finish(): mean_grad = jnp.mean(normed_grad, axis=1, keepdims=True)]
where the time goes in v3:
time: 76.2 us; the launch traced here: 75.6 us
  Pallas kernels  58.5 us (77%)
  other arithmetic  7.26 us (10%)
  local copies, waits for them, and re-layouts  5.46 us (7%)
  matrix products  3.52 us (5%)
  between operations  0.82 us (1%)
    pallas_call x1, Pallas kernels, middle(): pl.pallas_call(functools.partial(middle_kernel, lines), out_shape=tuple((...  31.1 us
    pallas_call x1, Pallas kernels, reduce_blocks(): pl.pallas_call(functools.partial(reduce_kernel, lines), out_shape=jax.Sha...  18.7 us
    pallas_call x1, Pallas kernels, weight_products(): pl.pallas_call(product_kernel, grid=(features // width,), out_shape=(shap...  8.76 us
    dot_general x1, matrix products, per_device(): jnp.dot(choose, terms, preferred_element_type=jnp.float32)  1.96 us
    dot_general x1, matrix products, per_device(): jnp.dot(my_hot, modulation[:, 1, :], precision=lax.Precision.HIGHEST)  1.56 us

profile of v3, /device:TPU:0, one launch (start us, length us, event | category | flops | bytes accessed | tf_op | source)
XLA Modules:
  0.0 75.6 jit_solution(16109880219467594660)
XLA Ops:
  0.6 0.8 %select_reduce_fusion = s32[64]{0:T(128)S(1)} fusion(s32[21]{0:T(128)} %param.22, s32[64]{0:T(128)} %param.21), kind=kLoop, calls=%fused_computation.31 | loop fusion | flops 3968 | bytes 596 | tf_op jit(solution)/shard_map/reduce_sum | solution.py:413
  1.4 0.1 dynamic_slice.6
  1.5 0.9 %convert_reduce_fusion = f32[4]{0:T(128)S(1)} fusion(bf16[4,5120]{1,0:T(4,128)(2,1)} %param.14), kind=kLoop, calls=%fused_computation.14 | loop fusion | flops 40956 | bytes 40976 | tf_op jit(solution)/shard_map/reduce_sum | solution.py:17
  2.4 1.0 %fusion.18 = f32[4]{0:T(128)S(1)} fusion(bf16[4,5120]{1,0:T(4,128)(2,1)} %param.14, f32[4]{0:T(128)S(1)} %broadcast_multiply_fusion.1), kind=kLoop, calls=%fused_computation.24 | loop fusion | flops 81916 | bytes 40992 | tf_op jit(solution)/shard_map/reduce_sum | solution.py:18
  3.4 0.7 iota_compare_fusion
  4.1 1.3 %broadcast_in_dim.19.bias_ref = f32[1,864]{1,0:T(1,128)} reshape(f32[864]{0:T(1024)} %param.19) | data formatting | bytes 6912 | tf_op jit(solution)/shard_map/broadcast_in_dim | solution.py:235
  5.4 0.8 %broadcast_compare_fusion = pred[160,4]{1,0:T(32,128)(4,1)S(1)} fusion(s32[4]{0:T(128)S(1)} %dynamic_slice.6, s32[160]{0:T(256)} %constant.44), kind=kLoop, calls=%fused_computation.29 | loop fusion | flops 640 | bytes 1296 | tf_op jit(solution)/shard_map/eq | solution.py:442
  6.1 1.4 %copy.28.ids_ref = s32[64,1]{1,0:T(8,128)} copy(s32[64,1]{0,1:T(1,128)} %bitcast.27) | data formatting | bytes 512 | tf_op jit(solution)/shard_map/broadcast_in_dim | solution.py:412
  7.5 0.9 %compare_or_fusion = (pred[160,64]{1,0:T(32,128)(4,1)S(1)}, pred[160,64]{1,0:T(32,128)(4,1)S(1)}) fusion(pred[160,64]{1,0:T(32,128)(4,1)} %constant.34.clone, s32[64]{0:T(128)S(1)} %select_reduce_fusion, s32[160]{0:T(256)} %constant.42, s32[160]{0:T(256)} %constant.43), kind=kLoop, calls=%fused_computation.28 | loop fusion | flops 30720 | bytes 32256 | tf_op jit(solution)/shard_map/or | solution.py:439
  8.4 0.8 %fusion.19 = bf16[4,5120]{1,0:T(4,128)(2,1)S(1)} fusion(bf16[4,5120]{1,0:T(4,128)(2,1)} %param.15, bf16[4,5120]{1,0:T(4,128)(2,1)} %param.16), kind=kLoop, calls=%fused_computation.25 | loop fusion | flops 81920 | bytes 122880 | tf_op jit(solution)/shard_map/convert_element_type | solution.py:450
  9.2 0.8 %fusion.26 = (bf16[4,2560]{1,0:T(4,128)(2,1)S(1)}, bf16[4,2560]{1,0:T(4,128)(2,1)S(1)}, bf16[4,2560]{1,0:T(4,128)(2,1)S(1)}, bf16[4,2560]{1,0:T(4,128)(2,1)S(1)}) fusion(bf16[4,5120]{1,0:T(4,128)(2,1)} %param.14, bf16[4,5120]{1,0:T(4,128)(2,1)} %param.15), kind=kLoop, calls=%fused_computation.42 | loop fusion | bytes 163840 | tf_op jit(solution)/shard_map/slice | solution.py:416
  10.0 0.7 pad_maximum_fusion.mine_ref
  10.7 31.1 %gather_and_middle.1 = (bf16[64,5120]{1,0:T(8,128)(2,1)}, bf16[64,5120]{1,0:T(8,128)(2,1)}, bf16[64,864]{1,0:T(8,128)(2,1)}, bf16[64,864]{1,0:T(8,128)(2,1)}, bf16[128,5120]{1,0:T(8,128)(2,1)}) custom-call(bf16[16,2560]{1,0:T(8,128)(2,1)} %pad_maximum_fusion.mine_ref, bf16[4,64,256]{2,1,0:T(8,128)(2,1)} %constant.32.clone.pick_ref, s32[64,1]{1,0:T(8,128)} %copy.28.ids_ref, ...), custom_call_target="tpu_custom_call" | custom-call | tf_op jit(solution)/shard_map/gather_and_middle/pallas_call | solution.py:209
  41.8 2.0 %convolution_convert_fusion = bf16[160,5120]{1,0:T(8,128)(2,1)S(1)} fusion(bf16[4,5120]{1,0:T(4,128)(2,1)S(1)} %fusion.19, bf16[128,5120]{1,0:T(8,128)(2,1)} %get-tuple-element.11, pred[160,4]{1,0:T(32,128)(4,1)S(1)} %broadcast_compare_fusion, pred[160,64]{1,0:T(32,128)(4,1)S(1)} %get-tuple-element.25, pred[160,64]{1,0:T(32,128)(4,1)S(1)} %get-tuple-element.24), kind=kOutput, calls=%fused_computation | convolution fusion | flops 219833600 | bytes 3011200 | tf_op jit(solution)/shard_map/dot_general | solution.py:454
  43.8 0.3 copy.32
  44.0 0.6 copy.29
  44.7 0.2 copy.30.parts_ref
  44.9 0.0 copy-start.4
  44.9 0.0 copy-start.5
  44.9 18.7 %reduce_rows.1 = f32[80,640]{1,0:T(8,128)S(1)} custom-call(bf16[2,2,4,80,640]{4,3,2,1,0:T(8,128)(2,1)S(1)} %copy.30.parts_ref), custom_call_target="tpu_custom_call" | custom-call | tf_op jit(solution)/shard_map/reduce_rows/pallas_call | solution.py:335
  63.6 0.0 copy-start
  63.6 0.0 copy-start.1
  63.6 0.0 copy-start.2
  63.7 0.0 copy-start.3
  63.8 0.7 reshape.51
  64.5 0.0 copy-done.4
  64.5 1.6 %fusion.25 = (f32[4]{0:T(128)S(1)}, f32[4]{0:T(128)S(1)}, f32[4,5120]{1,0:T(4,128)S(1)}) fusion(f32[4]{0:T(128)S(1)} %add_rsqrt_fusion, f32[4]{0:T(128)S(1)} %broadcast_multiply_fusion.1, bf16[4,5120]{1,0:T(4,128)(2,1)S(1)} %copy-done.4, f32[4,5120]{1,0:T(4,128)S(1)} %bitcast.25, f32[21,3,5120]{2,0,1:T(8,128)} %param.17, ...), kind=kOutput, calls=%fused_computation.41 | convolution fusion | flops 5324792 | bytes 697732 | tf_op jit(solution)/shard_map/dot_general | solution.py:466
  66.1 0.0 copy-done.5
  66.1 0.7 fusion.20
  66.8 0.0 copy-done
  66.8 0.0 copy-done.1
  66.8 0.0 copy-done.2
  66.8 0.0 copy-done.3
  66.8 8.8 %weight_products.1 = (bf16[864,5120]{1,0:T(8,128)(2,1)}, bf16[864,5120]{1,0:T(8,128)(2,1)}) custom-call(bf16[64,864]{1,0:T(8,128)(2,1)S(1)} %copy-done.2, bf16[64,5120]{1,0:T(8,128)(2,1)S(1)} %copy-done.1, bf16[64,864]{1,0:T(8,128)(2,1)S(1)} %copy-done.3, bf16[64,5120]{1,0:T(8,128)(2,1)S(1)} %copy-done), custom_call_target="tpu_custom_call" | custom-call | tf_op jit(solution)/shard_map/weight_products/pallas_call | solution.py:380
  (8 shorter events, 0.1 us)
Async XLA Ops:
  44.9 19.6 %copy-start.4 = (bf16[4,5120]{1,0:T(4,128)(2,1)S(1)}, bf16[4,5120]{1,0:T(4,128)(2,1)}, u32[]{:S(2)}) copy-start(bf16[4,5120]{1,0:T(4,128)(2,1)} %param.14) | copy-start | bytes 122884
  44.9 21.2 %copy-start.5 = (bf16[4,5120]{1,0:T(4,128)(2,1)S(1)}, bf16[4,5120]{1,0:T(4,128)(2,1)}, u32[]{:S(2)}) copy-start(bf16[4,5120]{1,0:T(4,128)(2,1)} %param.15) | copy-start | bytes 122884
  63.6 3.2 %copy-start = (bf16[64,5120]{1,0:T(8,128)(2,1)S(1)}, bf16[64,5120]{1,0:T(8,128)(2,1)}, u32[]{:S(2)}) copy-start(bf16[64,5120]{1,0:T(8,128)(2,1)} %get-tuple-element.15.modulated_ref) | copy-start | bytes 1966084
  63.6 3.2 %copy-start.1 = (bf16[64,5120]{1,0:T(8,128)(2,1)S(1)}, bf16[64,5120]{1,0:T(8,128)(2,1)}, u32[]{:S(2)}) copy-start(bf16[64,5120]{1,0:T(8,128)(2,1)} %get-tuple-element.13.gated_ref) | copy-start | bytes 1966084
  63.6 3.2 %copy-start.2 = (bf16[64,864]{1,0:T(8,128)(2,1)S(1)}, bf16[64,864]{1,0:T(8,128)(2,1)}, u32[]{:S(2)}) copy-start(bf16[64,864]{1,0:T(8,128)(2,1)} %get-tuple-element.12.activated_ref) | copy-start | bytes 331780
  63.7 3.2 %copy-start.3 = (bf16[64,864]{1,0:T(8,128)(2,1)S(1)}, bf16[64,864]{1,0:T(8,128)(2,1)}, u32[]{:S(2)}) copy-start(bf16[64,864]{1,0:T(8,128)(2,1)} %get-tuple-element.14.hidden_ref) | copy-start | bytes 331780

commit v4 on v3

--- a/solution.py
+++ b/solution.py
@@ -12,13 +12,6 @@
 MESH = pl.DeviceIdType.MESH
 
 
-def normalize(inputs):
-    values = inputs.astype(jnp.float32)
-    centred = values - jnp.mean(values, axis=1, keepdims=True)
-    inverse_std = lax.rsqrt(jnp.mean(centred * centred, axis=1, keepdims=True) + EPSILON)
-    return (centred * inverse_std, inverse_std)
-
-
 def position(lines):
     me = lax.axis_index("seq")
     return me, me // 4, (me // 2) % 2, me % 2
@@ -43,7 +36,7 @@
     lines,
     mine_ref,
     pick_ref,
-    ids_ref,
+    one_hot_ref,
     modulation_ref,
     in_weight_hbm,
     bias_ref,
@@ -53,6 +46,7 @@
     activated_ref,
     hidden_ref,
     terms_ref,
+    stats_ref,
     all_ref,
     in_weight_ref,
     out_weight_ref,
@@ -97,6 +91,22 @@
     send(mine_ref, me, side_send.at[0], device(line, 1 - side, core))
     send(mine_ref, me, core_send.at[0], device(line, side, 1 - core))
     all_ref[me] = mine_ref[...]
+
+    half_rows = mine_ref.shape[0] // 2
+    width = 2 * mine_ref.shape[1]
+    own = mine_ref[...].astype(jnp.float32)
+    first, second = own[:half_rows], own[half_rows:]
+    own_mean = (
+        jnp.sum(first, axis=1, keepdims=True) + jnp.sum(second, axis=1, keepdims=True)
+    ) / width
+    first, second = first - own_mean, second - own_mean
+    variance = (
+        jnp.sum(first * first, axis=1, keepdims=True)
+        + jnp.sum(second * second, axis=1, keepdims=True)
+    ) / width
+    stats_ref[:half_rows] = jnp.broadcast_to(own_mean, (half_rows, 128))
+    stats_ref[half_rows:] = jnp.broadcast_to(lax.rsqrt(variance + EPSILON), (half_rows, 128))
+
     for step in range(1, lines):
         block = (((line - step + lines) % lines) * 2 + side) * 2 + core
         arrived(block)
@@ -116,8 +126,7 @@
     total_rows, features = tokens_ref.shape
     width = half // 2
     flat = all_ref[...].reshape(n * block_rows, half)
-    frames = lax.broadcasted_iota(jnp.int32, (total_rows, modulation_ref.shape[1]), 1)
-    one_hot = (ids_ref[...] == frames).astype(jnp.float32).astype(jnp.bfloat16)
+    one_hot = one_hot_ref[...].astype(jnp.bfloat16)
 
     def picked(which, column):
         place = column % half
@@ -166,7 +175,7 @@
             across_last,
             preferred_element_type=jnp.float32,
         )
-        + bias_ref[...]
+        + bias_ref[...][None, :]
     )
     root = np.float32(np.sqrt(2.0 / np.pi))
     cubic = np.float32(0.044715)
@@ -193,9 +202,9 @@
         ).astype(jnp.bfloat16)
 
 
-def middle(block, pick, frame_ids, modulation, in_weight, in_bias, out_weight, n):
+def middle(block, pick, one_hot, modulation, in_weight, in_bias, out_weight, n):
     lines = n // 4
-    total_rows = frame_ids.shape[0]
+    total_rows = one_hot.shape[0]
     hidden, features = in_weight.shape
     vmem = pl.BlockSpec(memory_space=pltpu.VMEM)
     hbm = pl.BlockSpec(memory_space=pl.ANY)
@@ -208,9 +217,10 @@
     )
     return pl.pallas_call(
         functools.partial(middle_kernel, lines),
-        out_shape=tuple(jax.ShapeDtypeStruct(shape, jnp.bfloat16) for shape in shapes),
+        out_shape=tuple(jax.ShapeDtypeStruct(shape, jnp.bfloat16) for shape in shapes)
+        + (jax.ShapeDtypeStruct((block.shape[0], 128), jnp.float32),),
         in_specs=[vmem, vmem, vmem, vmem, hbm, vmem, hbm],
-        out_specs=(vmem,) * 5,
+        out_specs=(vmem,) * 6,
         scratch_shapes=[
             pltpu.VMEM((n,) + block.shape, block.dtype),
             pltpu.VMEM((hidden, features), jnp.bfloat16),
@@ -229,10 +239,10 @@
     )(
         block,
         pick,
-        frame_ids[:, None],
+        one_hot,
         modulation.transpose(1, 0, 2),
         in_weight,
-        in_bias[None, :],
+        in_bias,
         out_weight,
     )
 
@@ -417,8 +427,8 @@
     source = np.arange(total_rows) // rows * 4 * rows + np.arange(total_rows) % rows
     pick = np.stack([source + kind * rows for kind in range(4)])[:, :, None]
     pick = jnp.asarray(pick == np.arange(4 * total_rows), jnp.bfloat16)
-    modulated, gated_grad, activated, hidden_grad, terms = middle(
-        mine, pick, frame_ids, modulation, in_weight.T, in_bias, out_weight, n
+    modulated, gated_grad, activated, hidden_grad, terms, stats = middle(
+        mine, pick, one_hot, modulation, in_weight.T, in_bias, out_weight, n
     )
 
     per_owner = (frame_count + n - 1) // n
@@ -464,7 +474,8 @@
     mod_grad = sums[:rows]
     my_hot = lax.dynamic_slice_in_dim(one_hot, row_base, rows, 0)
     my_scale = jnp.dot(my_hot, modulation[:, 1, :], precision=lax.Precision.HIGHEST)
-    my_normed, my_inverse_std = normalize(tokens)
+    my_inverse_std = stats[2 * rows : 3 * rows, :1]
+    my_normed = (tokens.astype(jnp.float32) - stats[:rows, :1]) * my_inverse_std
     token_grad = finish(mod_grad, my_normed, my_inverse_std, my_scale, out_grad)
     frame_grads = sums[rows : rows + 3 * per_owner].reshape(3, per_owner, features)
     return (token_grad, in_weight_grad, out_weight_grad, frame_grads.transpose(1, 0, 2))

time: 76.2 us -> 73 us (0.958)
  local copies, waits for them, and re-layouts: 5.46 us -> 3.66 us
  other arithmetic: 7.26 us -> 6.09 us
    broadcast_in_dim x2 -> x0, local copies, waits for them, and re-layouts: 2.63 us -> none  [the longest x1 1.36 us: per_device(): frame_ids[:, None] == jnp.arange(frame_count, dtype=jnp.int32)[None, :]]
    reduce_sum x2 -> x0, other arithmetic: 1.94 us -> none  [the longest x1 1 us: normalize(): jnp.mean(centred * centred, axis=1, keepdims=True) + EPSILON]
    slice x0 -> x1, local copies, waits for them, and re-layouts: none -> 0.82 us  [per_device(): my_normed = (tokens.astype(jnp.float32) - stats[:rows, :1]) * my_inverse_std]
where the time goes in v4:
time: 73 us; the launch traced here: 72.6 us
  Pallas kernels  58.6 us (80%)
  other arithmetic  6.09 us (8%)
  local copies, waits for them, and re-layouts  3.66 us (5%)
  matrix products  3.43 us (5%)
  between operations  0.82 us (1%)
    pallas_call x1, Pallas kernels, middle(): pl.pallas_call(functools.partial(middle_kernel, lines), out_shape=tuple((...  31.1 us
    pallas_call x1, Pallas kernels, reduce_blocks(): pl.pallas_call(functools.partial(reduce_kernel, lines), out_shape=jax.Sha...  18.7 us
    pallas_call x1, Pallas kernels, weight_products(): pl.pallas_call(product_kernel, grid=(features // width,), out_shape=(shap...  8.76 us
    dot_general x1, matrix products, per_device(): jnp.dot(choose, terms, preferred_element_type=jnp.float32)  1.97 us
    dot_general x1, matrix products, per_device(): jnp.dot(my_hot, modulation[:, 1, :], precision=lax.Precision.HIGHEST)  1.46 us

profile of v4, /device:TPU:0, one launch (start us, length us, event | category | flops | bytes accessed | tf_op | source)
XLA Modules:
  0.0 72.6 jit_solution(698168832630151023)
XLA Ops:
  0.6 0.8 %select_reduce_fusion = s32[64]{0:T(128)S(1)} fusion(s32[21]{0:T(128)} %param.22, s32[64]{0:T(128)} %param.21), kind=kLoop, calls=%fused_computation.23 | loop fusion | flops 3968 | bytes 596 | tf_op jit(solution)/shard_map/reduce_sum | solution.py:423
  1.5 0.1 dynamic_slice.6
  1.6 0.8 %broadcast_compare_fusion = pred[160,4]{1,0:T(32,128)(4,1)S(1)} fusion(s32[4]{0:T(128)S(1)} %dynamic_slice.6, s32[160]{0:T(256)} %constant.40), kind=kLoop, calls=%fused_computation.21 | loop fusion | flops 640 | bytes 1296 | tf_op jit(solution)/shard_map/eq | solution.py:452
  2.3 0.9 %compare_or_fusion = (pred[160,64]{1,0:T(32,128)(4,1)S(1)}, pred[160,64]{1,0:T(32,128)(4,1)S(1)}) fusion(pred[160,64]{1,0:T(32,128)(4,1)} %constant.30.clone, s32[64]{0:T(128)S(1)} %select_reduce_fusion, s32[160]{0:T(256)} %constant.38, s32[160]{0:T(256)} %constant.39), kind=kLoop, calls=%fused_computation.20 | loop fusion | flops 30720 | bytes 32256 | tf_op jit(solution)/shard_map/or | solution.py:449
  3.2 0.8 %fusion.11 = bf16[4,5120]{1,0:T(4,128)(2,1)S(1)} fusion(bf16[4,5120]{1,0:T(4,128)(2,1)} %param.15, bf16[4,5120]{1,0:T(4,128)(2,1)} %param.16), kind=kLoop, calls=%fused_computation.15 | loop fusion | flops 81920 | bytes 122880 | tf_op jit(solution)/shard_map/convert_element_type | solution.py:460
  4.0 1.3 %iota_compare_fusion = (pred[64,21]{1,0:T(8,128)(4,1)S(1)}, f32[64,21]{1,0:T(8,128)}) fusion(s32[64]{0:T(128)} %param.21), kind=kLoop, calls=%fused_computation.24 | loop fusion | flops 2688 | bytes 6976 | tf_op jit(solution)/shard_map/eq | solution.py:422
  5.4 0.8 %fusion.19 = (bf16[4,2560]{1,0:T(4,128)(2,1)S(1)}, bf16[4,2560]{1,0:T(4,128)(2,1)S(1)}, bf16[4,2560]{1,0:T(4,128)(2,1)S(1)}, bf16[4,2560]{1,0:T(4,128)(2,1)S(1)}) fusion(bf16[4,5120]{1,0:T(4,128)(2,1)} %param.14, bf16[4,5120]{1,0:T(4,128)(2,1)} %param.15), kind=kLoop, calls=%fused_computation.35 | loop fusion | bytes 163840 | tf_op jit(solution)/shard_map/slice | solution.py:426
  6.2 0.7 pad_maximum_fusion.mine_ref
  6.9 31.1 %gather_and_middle.1 = (bf16[64,5120]{1,0:T(8,128)(2,1)}, bf16[64,5120]{1,0:T(8,128)(2,1)}, bf16[64,864]{1,0:T(8,128)(2,1)}, bf16[64,864]{1,0:T(8,128)(2,1)}, bf...) custom-call(bf16[16,2560]{1,0:T(8,128)(2,1)} %pad_maximum_fusion.mine_ref, bf16[4,64,256]{2,1,0:T(8,128)(2,1)} %constant.28.clone.pick_ref, ...), custom_call_target="tpu_custom_call" | custom-call | tf_op jit(solution)/shard_map/gather_and_middle/pallas_call | solution.py:218
  38.0 0.8 %slice_reduce_fusion.1 = (f32[4]{0:T(128)S(1)}, f32[4]{0:T(128)S(1)}) fusion(f32[16,128]{1,0:T(8,128)} %get-tuple-element.13), kind=kLoop, calls=%fused_computation.27 | loop fusion | bytes 64 | tf_op jit(solution)/shard_map/slice | solution.py:478
  38.8 2.0 %convolution_convert_fusion = bf16[160,5120]{1,0:T(8,128)(2,1)S(1)} fusion(bf16[4,5120]{1,0:T(4,128)(2,1)S(1)} %fusion.11, bf16[128,5120]{1,0:T(8,128)(2,1)} %get-tuple-element.12, pred[160,4]{1,0:T(32,128)(4,1)S(1)} %broadcast_compare_fusion, pred[160,64]{1,0:T(32,128)(4,1)S(1)} %get-tuple-element.31, pred[160,64]{1,0:T(32,128)(4,1)S(1)} %get-tuple-element.30), kind=kOutput, calls=%fused_computation | convolution fusion | flops 219833600 | bytes 3011200 | tf_op jit(solution)/shard_map/dot_general | solution.py:464
  40.8 0.3 copy.25
  41.1 0.6 copy.22
  41.7 0.2 copy.23.parts_ref
  41.9 0.0 copy-start.5
  41.9 0.0 copy-start.4
  42.0 18.7 %reduce_rows.1 = f32[80,640]{1,0:T(8,128)S(1)} custom-call(bf16[2,2,4,80,640]{4,3,2,1,0:T(8,128)(2,1)S(1)} %copy.23.parts_ref), custom_call_target="tpu_custom_call" | custom-call | tf_op jit(solution)/shard_map/reduce_rows/pallas_call | solution.py:345
  60.7 0.0 copy-start
  60.7 0.0 copy-start.1
  60.7 0.0 copy-start.2
  60.7 0.0 copy-start.3
  60.8 0.7 reshape.39
  61.5 0.0 copy-done.5
  61.5 1.5 %fusion.18 = (f32[4]{0:T(128)S(1)}, f32[4]{0:T(128)S(1)}, f32[4,5120]{1,0:T(4,128)S(1)}) fusion(f32[4]{0:T(128)S(1)} %get-tuple-element.23, f32[4]{0:T(128)S(1)} %get-tuple-element.22, bf16[4,5120]{1,0:T(4,128)(2,1)S(1)} %copy-done.5, f32[4,5120]{1,0:T(4,128)S(1)} %bitcast.24, f32[21,3,5120]{2,0,1:T(8,128)} %param.17, ...), kind=kOutput, calls=%fused_computation.34 | convolution fusion | flops 5324792 | bytes 697892 | tf_op jit(solution)/shard_map/dot_general | solution.py:476
  63.0 0.0 copy-done.4
  63.0 0.7 %fusion.12 = bf16[4,5120]{1,0:T(4,128)(2,1)} fusion(bf16[4,5120]{1,0:T(4,128)(2,1)S(1)} %copy-done.4, bf16[4,5120]{1,0:T(4,128)(2,1)S(1)} %copy-done.5, f32[4,5120]{1,0:T(4,128)S(1)} %get-tuple-element.32, f32[4]{0:T(128)S(1)} %broadcast_multiply_fusion, f32[4]{0:T(128)S(1)} %get-tuple-element.23, f32[4]{0:T(128)S(1)} %get-tuple-element.22, ...), kind=kLoop, calls=%fused_computation.16 | loop fusion | flops 204800 | bytes 204864 | tf_op jit(solution)/shard_map/convert_element_type | solution.py:408
  63.8 0.0 copy-done
  63.8 0.0 copy-done.1
  63.8 0.0 copy-done.2
  63.8 0.0 copy-done.3
  63.8 8.8 %weight_products.1 = (bf16[864,5120]{1,0:T(8,128)(2,1)}, bf16[864,5120]{1,0:T(8,128)(2,1)}) custom-call(bf16[64,864]{1,0:T(8,128)(2,1)S(1)} %copy-done.2, bf16[64,5120]{1,0:T(8,128)(2,1)S(1)} %copy-done.1, bf16[64,864]{1,0:T(8,128)(2,1)S(1)} %copy-done.3, bf16[64,5120]{1,0:T(8,128)(2,1)S(1)} %copy-done), custom_call_target="tpu_custom_call" | custom-call | tf_op jit(solution)/shard_map/weight_products/pallas_call | solution.py:390
  (6 shorter events, 0.1 us)
Async XLA Ops:
  41.9 19.6 %copy-start.5 = (bf16[4,5120]{1,0:T(4,128)(2,1)S(1)}, bf16[4,5120]{1,0:T(4,128)(2,1)}, u32[]{:S(2)}) copy-start(bf16[4,5120]{1,0:T(4,128)(2,1)} %param.14) | copy-start | bytes 122884
  41.9 21.1 %copy-start.4 = (bf16[4,5120]{1,0:T(4,128)(2,1)S(1)}, bf16[4,5120]{1,0:T(4,128)(2,1)}, u32[]{:S(2)}) copy-start(bf16[4,5120]{1,0:T(4,128)(2,1)} %param.15) | copy-start | bytes 122884
  60.7 3.1 %copy-start = (bf16[64,5120]{1,0:T(8,128)(2,1)S(1)}, bf16[64,5120]{1,0:T(8,128)(2,1)}, u32[]{:S(2)}) copy-start(bf16[64,5120]{1,0:T(8,128)(2,1)} %get-tuple-element.17.modulated_ref) | copy-start | bytes 1966084
  60.7 3.1 %copy-start.1 = (bf16[64,5120]{1,0:T(8,128)(2,1)S(1)}, bf16[64,5120]{1,0:T(8,128)(2,1)}, u32[]{:S(2)}) copy-start(bf16[64,5120]{1,0:T(8,128)(2,1)} %get-tuple-element.15.gated_ref) | copy-start | bytes 1966084
  60.7 3.1 %copy-start.2 = (bf16[64,864]{1,0:T(8,128)(2,1)S(1)}, bf16[64,864]{1,0:T(8,128)(2,1)}, u32[]{:S(2)}) copy-start(bf16[64,864]{1,0:T(8,128)(2,1)} %get-tuple-element.14.activated_ref) | copy-start | bytes 331780
  60.7 3.1 %copy-start.3 = (bf16[64,864]{1,0:T(8,128)(2,1)S(1)}, bf16[64,864]{1,0:T(8,128)(2,1)}, u32[]{:S(2)}) copy-start(bf16[64,864]{1,0:T(8,128)(2,1)} %get-tuple-element.16.hidden_ref) | copy-start | bytes 331780

commit v5 on v4

--- a/solution.py
+++ b/solution.py
@@ -51,6 +51,7 @@
     in_weight_ref,
     out_weight_ref,
     tokens_ref,
+    rows_ref,
     line_send,
     side_send,
     core_send,
@@ -92,6 +93,23 @@
     send(mine_ref, me, core_send.at[0], device(line, side, 1 - core))
     all_ref[me] = mine_ref[...]
 
+    one_hot = one_hot_ref[...].astype(jnp.bfloat16)
+    part = mine_ref.shape[1] // 2
+
+    def spread_rows(which, column):
+        values = modulation_ref[which, :, column : column + part]
+        high = values.astype(jnp.bfloat16)
+        rest = values - high.astype(jnp.float32)
+        low = rest.astype(jnp.bfloat16)
+        lowest = (rest - low.astype(jnp.float32)).astype(jnp.bfloat16)
+        total = jnp.dot(one_hot, lowest, preferred_element_type=jnp.float32)
+        total = total + jnp.dot(one_hot, low, preferred_element_type=jnp.float32)
+        return total + jnp.dot(one_hot, high, preferred_element_type=jnp.float32)
+
+    for which in range(3):
+        for column in range(0, rows_ref.shape[2], part):
+            rows_ref[which, :, column : column + part] = spread_rows(which, column)
+
     half_rows = mine_ref.shape[0] // 2
     width = 2 * mine_ref.shape[1]
     own = mine_ref[...].astype(jnp.float32)
@@ -126,7 +144,6 @@
     total_rows, features = tokens_ref.shape
     width = half // 2
     flat = all_ref[...].reshape(n * block_rows, half)
-    one_hot = one_hot_ref[...].astype(jnp.bfloat16)
 
     def picked(which, column):
         place = column % half
@@ -137,14 +154,7 @@
         )
 
     def spread(which, column):
-        values = modulation_ref[which, :, column : column + width]
-        high = values.astype(jnp.bfloat16)
-        rest = values - high.astype(jnp.float32)
-        low = rest.astype(jnp.bfloat16)
-        lowest = (rest - low.astype(jnp.float32)).astype(jnp.bfloat16)
-        total = jnp.dot(one_hot, lowest, preferred_element_type=jnp.float32)
-        total = total + jnp.dot(one_hot, low, preferred_element_type=jnp.float32)
-        return total + jnp.dot(one_hot, high, preferred_element_type=jnp.float32)
+        return rows_ref[which, :, column : column + width]
 
     columns = range(0, features, width)
     total = jnp.zeros((total_rows, 1), jnp.float32)
@@ -226,6 +236,7 @@
             pltpu.VMEM((hidden, features), jnp.bfloat16),
             pltpu.VMEM((hidden, features), jnp.bfloat16),
             pltpu.VMEM((total_rows, features), jnp.float32),
+            pltpu.VMEM((3, total_rows, features), jnp.float32),
             pltpu.SemaphoreType.DMA((lines,)),
             pltpu.SemaphoreType.DMA((lines,)),
             pltpu.SemaphoreType.DMA((2 * lines,)),

time: 73 us -> 71.8 us (0.984)
  Pallas kernels: 58.6 us -> 57.3 us
    pallas_call x1, Pallas kernels: 31.1 us -> 29.9 us  [middle(): pl.pallas_call(functools.partial(middle_kernel, lines), out_shape=tuple((...]
where the time goes in v5:
time: 71.8 us; the launch traced here: 71.3 us
  Pallas kernels  57.3 us (80%)
  other arithmetic  6.09 us (8%)
  local copies, waits for them, and re-layouts  3.66 us (5%)
  matrix products  3.43 us (5%)
  between operations  0.82 us (1%)
    pallas_call x1, Pallas kernels, middle(): pl.pallas_call(functools.partial(middle_kernel, lines), out_shape=tuple((...  29.9 us
    pallas_call x1, Pallas kernels, reduce_blocks(): pl.pallas_call(functools.partial(reduce_kernel, lines), out_shape=jax.Sha...  18.7 us
    pallas_call x1, Pallas kernels, weight_products(): pl.pallas_call(product_kernel, grid=(features // width,), out_shape=(shap...  8.76 us
    dot_general x1, matrix products, per_device(): jnp.dot(choose, terms, preferred_element_type=jnp.float32)  1.97 us
    dot_general x1, matrix products, per_device(): jnp.dot(my_hot, modulation[:, 1, :], precision=lax.Precision.HIGHEST)  1.46 us

profile of v5, /device:TPU:0, one launch (start us, length us, event | category | flops | bytes accessed | tf_op | source)
XLA Modules:
  0.0 71.3 jit_solution(6688607011004672672)
XLA Ops:
  0.6 0.8 %select_reduce_fusion = s32[64]{0:T(128)S(1)} fusion(s32[21]{0:T(128)} %param.22, s32[64]{0:T(128)} %param.21), kind=kLoop, calls=%fused_computation.23 | loop fusion | flops 3968 | bytes 596 | tf_op jit(solution)/shard_map/reduce_sum | solution.py:434
  1.5 0.1 dynamic_slice.6
  1.6 0.8 %broadcast_compare_fusion = pred[160,4]{1,0:T(32,128)(4,1)S(1)} fusion(s32[4]{0:T(128)S(1)} %dynamic_slice.6, s32[160]{0:T(256)} %constant.40), kind=kLoop, calls=%fused_computation.21 | loop fusion | flops 640 | bytes 1296 | tf_op jit(solution)/shard_map/eq | solution.py:463
  2.3 0.9 %compare_or_fusion = (pred[160,64]{1,0:T(32,128)(4,1)S(1)}, pred[160,64]{1,0:T(32,128)(4,1)S(1)}) fusion(pred[160,64]{1,0:T(32,128)(4,1)} %constant.30.clone, s32[64]{0:T(128)S(1)} %select_reduce_fusion, s32[160]{0:T(256)} %constant.38, s32[160]{0:T(256)} %constant.39), kind=kLoop, calls=%fused_computation.20 | loop fusion | flops 30720 | bytes 32256 | tf_op jit(solution)/shard_map/or | solution.py:460
  3.2 0.8 %fusion.11 = bf16[4,5120]{1,0:T(4,128)(2,1)S(1)} fusion(bf16[4,5120]{1,0:T(4,128)(2,1)} %param.15, bf16[4,5120]{1,0:T(4,128)(2,1)} %param.16), kind=kLoop, calls=%fused_computation.15 | loop fusion | flops 81920 | bytes 122880 | tf_op jit(solution)/shard_map/convert_element_type | solution.py:471
  4.0 1.3 %iota_compare_fusion = (pred[64,21]{1,0:T(8,128)(4,1)S(1)}, f32[64,21]{1,0:T(8,128)}) fusion(s32[64]{0:T(128)} %param.21), kind=kLoop, calls=%fused_computation.24 | loop fusion | flops 2688 | bytes 6976 | tf_op jit(solution)/shard_map/eq | solution.py:433
  5.4 0.8 %fusion.19 = (bf16[4,2560]{1,0:T(4,128)(2,1)S(1)}, bf16[4,2560]{1,0:T(4,128)(2,1)S(1)}, bf16[4,2560]{1,0:T(4,128)(2,1)S(1)}, bf16[4,2560]{1,0:T(4,128)(2,1)S(1)}) fusion(bf16[4,5120]{1,0:T(4,128)(2,1)} %param.14, bf16[4,5120]{1,0:T(4,128)(2,1)} %param.15), kind=kLoop, calls=%fused_computation.35 | loop fusion | bytes 163840 | tf_op jit(solution)/shard_map/slice | solution.py:437
  6.2 0.7 pad_maximum_fusion.mine_ref
  6.9 29.9 %gather_and_middle.1 = (bf16[64,5120]{1,0:T(8,128)(2,1)}, bf16[64,5120]{1,0:T(8,128)(2,1)}, bf16[64,864]{1,0:T(8,128)(2,1)}, bf16[64,864]{1,0:T(8,128)(2,1)}, bf...) custom-call(bf16[16,2560]{1,0:T(8,128)(2,1)} %pad_maximum_fusion.mine_ref, bf16[4,64,256]{2,1,0:T(8,128)(2,1)} %constant.28.clone.pick_ref, ...), custom_call_target="tpu_custom_call" | custom-call | tf_op jit(solution)/shard_map/gather_and_middle/pallas_call | solution.py:228
  36.8 0.8 %slice_reduce_fusion.1 = (f32[4]{0:T(128)S(1)}, f32[4]{0:T(128)S(1)}) fusion(f32[16,128]{1,0:T(8,128)} %get-tuple-element.13), kind=kLoop, calls=%fused_computation.27 | loop fusion | bytes 64 | tf_op jit(solution)/shard_map/slice | solution.py:489
  37.6 2.0 %convolution_convert_fusion = bf16[160,5120]{1,0:T(8,128)(2,1)S(1)} fusion(bf16[4,5120]{1,0:T(4,128)(2,1)S(1)} %fusion.11, bf16[128,5120]{1,0:T(8,128)(2,1)} %get-tuple-element.12, pred[160,4]{1,0:T(32,128)(4,1)S(1)} %broadcast_compare_fusion, pred[160,64]{1,0:T(32,128)(4,1)S(1)} %get-tuple-element.31, pred[160,64]{1,0:T(32,128)(4,1)S(1)} %get-tuple-element.30), kind=kOutput, calls=%fused_computation | convolution fusion | flops 219833600 | bytes 3011200 | tf_op jit(solution)/shard_map/dot_general | solution.py:475
  39.6 0.3 copy.25
  39.8 0.6 copy.22
  40.5 0.2 copy.23.parts_ref
  40.7 0.0 copy-start.5
  40.7 0.0 copy-start.4
  40.7 18.7 %reduce_rows.1 = f32[80,640]{1,0:T(8,128)S(1)} custom-call(bf16[2,2,4,80,640]{4,3,2,1,0:T(8,128)(2,1)S(1)} %copy.23.parts_ref), custom_call_target="tpu_custom_call" | custom-call | tf_op jit(solution)/shard_map/reduce_rows/pallas_call | solution.py:356
  59.4 0.0 copy-start
  59.4 0.0 copy-start.1
  59.4 0.0 copy-start.2
  59.5 0.0 copy-start.3
  59.6 0.7 %reshape.39 = f32[3,2,5120]{2,1,0:T(2,128)} reshape(f32[6,8,640]{2,1,0:T(8,128)S(1)} %copy.24) | data formatting | bytes 245760 | tf_op jit(solution)/shard_map/reshape | solution.py:491
  60.3 0.0 copy-done.5
  60.3 1.5 %fusion.18 = (f32[4]{0:T(128)S(1)}, f32[4]{0:T(128)S(1)}, f32[4,5120]{1,0:T(4,128)S(1)}) fusion(f32[4]{0:T(128)S(1)} %get-tuple-element.23, f32[4]{0:T(128)S(1)} %get-tuple-element.22, bf16[4,5120]{1,0:T(4,128)(2,1)S(1)} %copy-done.5, f32[4,5120]{1,0:T(4,128)S(1)} %bitcast.24, f32[21,3,5120]{2,0,1:T(8,128)} %param.17, ...), kind=kOutput, calls=%fused_computation.34 | convolution fusion | flops 5324792 | bytes 697892 | tf_op jit(solution)/shard_map/dot_general | solution.py:487
  61.8 0.0 copy-done.4
  61.8 0.7 %fusion.12 = bf16[4,5120]{1,0:T(4,128)(2,1)} fusion(bf16[4,5120]{1,0:T(4,128)(2,1)S(1)} %copy-done.4, bf16[4,5120]{1,0:T(4,128)(2,1)S(1)} %copy-done.5, f32[4,5120]{1,0:T(4,128)S(1)} %get-tuple-element.32, f32[4]{0:T(128)S(1)} %broadcast_multiply_fusion, f32[4]{0:T(128)S(1)} %get-tuple-element.23, f32[4]{0:T(128)S(1)} %get-tuple-element.22, ...), kind=kLoop, calls=%fused_computation.16 | loop fusion | flops 204800 | bytes 204864 | tf_op jit(solution)/shard_map/convert_element_type | solution.py:419
  62.5 0.0 copy-done
  62.5 0.0 copy-done.1
  62.5 0.0 copy-done.2
  62.5 0.0 copy-done.3
  62.6 8.8 %weight_products.1 = (bf16[864,5120]{1,0:T(8,128)(2,1)}, bf16[864,5120]{1,0:T(8,128)(2,1)}) custom-call(bf16[64,864]{1,0:T(8,128)(2,1)S(1)} %copy-done.2, bf16[64,5120]{1,0:T(8,128)(2,1)S(1)} %copy-done.1, bf16[64,864]{1,0:T(8,128)(2,1)S(1)} %copy-done.3, bf16[64,5120]{1,0:T(8,128)(2,1)S(1)} %copy-done), custom_call_target="tpu_custom_call" | custom-call | tf_op jit(solution)/shard_map/weight_products/pallas_call | solution.py:401
  (6 shorter events, 0.1 us)
Async XLA Ops:
  40.7 19.6 %copy-start.5 = (bf16[4,5120]{1,0:T(4,128)(2,1)S(1)}, bf16[4,5120]{1,0:T(4,128)(2,1)}, u32[]{:S(2)}) copy-start(bf16[4,5120]{1,0:T(4,128)(2,1)} %param.14) | copy-start | bytes 122884
  40.7 21.1 %copy-start.4 = (bf16[4,5120]{1,0:T(4,128)(2,1)S(1)}, bf16[4,5120]{1,0:T(4,128)(2,1)}, u32[]{:S(2)}) copy-start(bf16[4,5120]{1,0:T(4,128)(2,1)} %param.15) | copy-start | bytes 122884
  59.4 3.1 %copy-start = (bf16[64,5120]{1,0:T(8,128)(2,1)S(1)}, bf16[64,5120]{1,0:T(8,128)(2,1)}, u32[]{:S(2)}) copy-start(bf16[64,5120]{1,0:T(8,128)(2,1)} %get-tuple-element.17.modulated_ref) | copy-start | bytes 1966084
  59.4 3.1 %copy-start.1 = (bf16[64,5120]{1,0:T(8,128)(2,1)S(1)}, bf16[64,5120]{1,0:T(8,128)(2,1)}, u32[]{:S(2)}) copy-start(bf16[64,5120]{1,0:T(8,128)(2,1)} %get-tuple-element.15.gated_ref) | copy-start | bytes 1966084
  59.4 3.1 %copy-start.2 = (bf16[64,864]{1,0:T(8,128)(2,1)S(1)}, bf16[64,864]{1,0:T(8,128)(2,1)}, u32[]{:S(2)}) copy-start(bf16[64,864]{1,0:T(8,128)(2,1)} %get-tuple-element.14.activated_ref) | copy-start | bytes 331780
  59.5 3.1 %copy-start.3 = (bf16[64,864]{1,0:T(8,128)(2,1)S(1)}, bf16[64,864]{1,0:T(8,128)(2,1)}, u32[]{:S(2)}) copy-start(bf16[64,864]{1,0:T(8,128)(2,1)} %get-tuple-element.16.hidden_ref) | copy-start | bytes 331780
